TPU v7x, 32 devices: a whole 2x2x4 slice. The times are simulated.
32 devices in a mesh: region: 4 (over z), bulk: 8 (over y, x, core).
Axes of the slice: x: 2, y: 2, z: 4, core: 2. Of those that a mesh axis runs over, the one named last changes fastest.
Arguments:
- positions: float32 [2048, 3, 128], P(('region', 'bulk')), may hold values from -6 to 6
- fields: float32 [2048, 4, 128], P(('region', 'bulk')), may hold values from -6 to 6
- storage: float32 [2048, 128], P(('region', 'bulk')), may hold values from 0.5 to 2
- velocity: float32 [2048, 3, 128], P(('region', 'bulk')), may hold values from -4 to 4
- send_list: int32 [32, 3, 8, 1], P(('region', 'bulk')), may hold values from 0 to 63
- remote_local: int32 [32, 24, 2], P(('region', 'bulk')), may hold values from 0 to 63
- remote_mask: int32 [32, 24, 2, 16, 128], P(('region', 'bulk')), may hold values from 0 to 255
- local_pairs: int32 [32, 64, 2], P(('region', 'bulk')), may hold values from 0 to 63, as said below
- local_mask: int32 [32, 64, 16, 128], P(('region', 'bulk')), may hold values from 0 to 255
- migrate_list: int32 [32, 8, 1], P(('region', 'bulk')), may hold values from -1 to 63, as said below
Outputs:
- new_fields: float32 [2048, 4, 128], P(('region', 'bulk'))
- new_velocity: float32 [2048, 3, 128], P(('region', 'bulk'))
- arrived: float32 [256, 11, 128], P(('region', 'bulk'))
Inputs may be any that keep to these rules, and one draw needn't show every extreme that they name: `local_pairs`: each pair names two different owned blocks. `migrate_list`: owned blocks named on one device are distinct; in each region some devices hand 1 blocks to each of several peers and the rest hand none.
All inputs are finite; a program needn't handle non-finite values.
Results may differ from a plain program's by a relative error of at most 0.00002.
Values sent between devices are 32-bit elements; how exact they have to be, the bound alone decides.
A program may use at most 64 MiB of HBM per device.

v0:
```python
import jax
import jax.numpy as jnp
from jax import lax
from jax.sharding import PartitionSpec as P

bond_stiff = 0.1
press_gain = 0.05
leak_gain = 0.5
time_step = 0.5
inv_horizon = 0.25
group_rows = 16


def from_behind(shard, axis, by):
    peers = lax.axis_size(axis)
    return lax.ppermute(shard, axis, [(i, (i + by) % peers) for i in range(peers)])


def unpack_bonds(packed):
    shifts = jnp.arange(8, dtype=jnp.int32)
    bit_table = jnp.bitwise_and(
        jnp.right_shift(packed[:, :, None, :], shifts[None, None, :, None]), 1
    )
    return bit_table.reshape(packed.shape[0], packed.shape[1] * 8, packed.shape[2]).astype(
        jnp.float32
    )


def tile_group(owned, others, packed):
    intact = unpack_bonds(packed)
    broken = 1.0 - intact
    apart = [others[:, k, :, None] - owned[:, k, None, :] for k in range(3)]
    dist_sq = apart[0] * apart[0] + apart[1] * apart[1] + apart[2] * apart[2]
    weight = 1.0 / (1.0 + inv_horizon * dist_sq)
    spring = bond_stiff * weight * intact
    leakage = weight * broken
    mean_press = 0.5 * (others[:, 6, :, None] + owned[:, 6, None, :])
    terms = [
        spring * (others[:, 3 + k, :, None] - owned[:, 3 + k, None, :])
        - press_gain * leakage * mean_press * apart[k]
        for k in range(3)
    ]
    terms.append(leak_gain * leakage * (others[:, 6, :, None] - owned[:, 6, None, :]))
    on_owned = jnp.stack([jnp.sum(t, axis=1) for t in terms], axis=1)
    on_others = jnp.stack([-jnp.sum(t, axis=2) for t in terms], axis=1)
    return (on_owned, on_others)


def tiles(owned, others, packed):
    count = owned.shape[0]
    groups = count // group_rows

    def one_group(items):
        return tile_group(items[0], items[1], items[2])

    on_owned, on_others = lax.map(
        one_group,
        (
            owned.reshape(groups, group_rows, 7, -1),
            others.reshape(groups, group_rows, 7, -1),
            packed.reshape(groups, group_rows, packed.shape[1], packed.shape[2]),
        ),
    )
    return (on_owned.reshape(count, 4, -1), on_others.reshape(count, 4, -1))


def per_device(
    positions,
    fields,
    storage,
    velocity,
    send_list,
    remote_local,
    remote_mask,
    local_pairs,
    local_mask,
    migrate_list,
):
    points = jnp.concatenate([positions, fields], axis=1)
    width = points.shape[2]
    nbulk = lax.axis_size("bulk")
    sends = send_list[0]
    slots = sends.shape[2]
    outgoing = points[sends.reshape(-1)].reshape(3, nbulk, slots, 7, width)
    spread = lax.all_to_all(outgoing, "bulk", split_axis=1, concat_axis=1, tiled=True)
    lifted = [from_behind(spread[offset + 1], "region", offset) for offset in (-1, 1)]
    received = jnp.stack([lifted[0], spread[1], lifted[1]])
    received = received.reshape(-1, 7, width)
    bonded = remote_local[0]
    slot_count, touch = bonded.shape
    flat_local = bonded.reshape(-1)
    others = jnp.broadcast_to(received[:, None], (slot_count, touch, 7, width)).reshape(
        -1, 7, width
    )
    masks = remote_mask[0]
    on_owned, on_others = tiles(
        points[flat_local],
        others,
        masks.reshape(slot_count * touch, masks.shape[2], masks.shape[3]),
    )
    totals = jnp.zeros((points.shape[0], 4, width), jnp.float32)
    totals = totals.at[flat_local].add(on_owned)
    slot_back = (
        on_others.reshape(slot_count, touch, 4, width)
        .sum(axis=1)
        .reshape(3, nbulk, slots, 4, width)
    )
    pairs = local_pairs[0]
    first_block = pairs[:, 0]
    second_block = pairs[:, 1]
    pair_first, pair_second = tiles(points[first_block], points[second_block], local_mask[0])
    totals = totals.at[first_block].add(pair_first).at[second_block].add(pair_second)
    lowered = [from_behind(slot_back[offset + 1], "region", -offset) for offset in (-1, 1)]
    stacked_back = jnp.stack([lowered[0], slot_back[1], lowered[1]])
    returned = lax.all_to_all(stacked_back, "bulk", split_axis=1, concat_axis=1, tiled=True)
    totals = totals.at[sends.reshape(-1)].add(returned.reshape(-1, 4, width))
    new_velocity = velocity + time_step * totals[:, :3]
    displace = fields[:, :3] + time_step * new_velocity
    pressure = fields[:, 3] + time_step * totals[:, 3] / storage
    new_fields = jnp.concatenate([displace, pressure[:, None, :]], axis=1)
    moving = jnp.concatenate([new_fields, new_velocity, positions, storage[:, None, :]], axis=1)
    moves = migrate_list[0]
    chosen = moving[jnp.maximum(moves, 0).reshape(-1)].reshape(
        moves.shape[0], moves.shape[1], 11, width
    )
    chosen = jnp.where((moves >= 0)[:, :, None, None], chosen, 0.0)
    arrived = lax.all_to_all(chosen, "bulk", split_axis=0, concat_axis=0, tiled=True)
    return (new_fields, new_velocity, arrived.reshape(-1, 11, width))


def solution(mesh):
    return jax.shard_map(
        per_device,
        mesh=mesh,
        in_specs=(
            P(("region", "bulk"), None, None),
            P(("region", "bulk"), None, None),
            P(("region", "bulk"), None),
            P(("region", "bulk"), None, None),
            P(("region", "bulk"), None, None, None),
            P(("region", "bulk"), None, None),
            P(("region", "bulk"), None, None, None, None),
            P(("region", "bulk"), None, None),
            P(("region", "bulk"), None, None, None),
            P(("region", "bulk"), None, None),
        ),
        out_specs=(
            P(("region", "bulk"), None, None),
            P(("region", "bulk"), None, None),
            P(("region", "bulk"), None, None),
        ),
        check_vma=False,
    )
```

profile of v0, /device:TPU:0, one launch (start us, length us, event | category | flops | bytes accessed | tf_op | source)
XLA Modules:
  0.0 102.4 jit_solution(15460132147548106155)
XLA Ops:
  0.6 1.0 copy.370
  3.1 0.7 copy.371
  3.8 5.2 %all-to-all-start = ((f32[3,8,1,7,128]{4,2,3,0,1:T(1,128)}), f32[3,8,1,7,128]{4,2,3,0,1:T(1,128)S(1)}, u32[]{:S(2)}, u32[]{:S(2)}) async-start(f32[3,8,1,7,128]{4,2,3,0,1:T(1,128)} %copy.371), calls=%async_computation | async-start | bytes 172032 | tf_op jit(solution)/shard_map/all_to_all | solution.py:85
  11.9 27.4 %while.25 = (s32[]{:T(128)}, f32[4,16,4,128]{3,1,0,2:T(8,128)S(1)}, f32[4,16,4,128]{3,1,0,2:T(8,128)S(1)}, f32[4,16,7,128]{3,2,1,0:T(8,128)S(1)}, f32[4,16,7,128...) while((s32[]{:T(128)}, f32[4,16,4,128]{3,1,0,2:T(8,128)S(1)}, ...), condition=%wide.region_20.21_spmd, body=%wide.region_11.20_spmd.sunk | while | flops 11837442 | bytes 1654877 | solution.py:56
  13.1 0.9 dynamic-slice_bitcast_fusion.11
  14.0 3.6 %fusion.49 = (f32[16,16,8]{2,1,0:T(8,128)S(1)}, f32[16,128]{1,0:T(8,128)S(1)}, f32[16,128]{1,0:T(8,128)S(1)}, f32[16,16,8]{2,1,0:T(8,128)S(1)}, f32[16,128]{1,0:...) fusion(f32[16,128]{1,0:T(8,128)S(1)} %get-tuple-element.434, ...), kind=kLoop, calls=%fused_computation.82.clone.1 | loop fusion | flops 11780096 | bytes 311296 | tf_op jit(solution)/shard_map/while/body/eval_jaxpr/reduce_sum | solution.py:45
  19.9 0.9 dynamic-slice_bitcast_fusion.11
  20.9 3.6 %fusion.49 = (f32[16,16,8]{2,1,0:T(8,128)S(1)}, f32[16,128]{1,0:T(8,128)S(1)}, f32[16,128]{1,0:T(8,128)S(1)}, f32[16,16,8]{2,1,0:T(8,128)S(1)}, f32[16,128]{1,0:...) fusion(f32[16,128]{1,0:T(8,128)S(1)} %get-tuple-element.434, ...), kind=kLoop, calls=%fused_computation.82.clone.1 | loop fusion | flops 11780096 | bytes 311296 | tf_op jit(solution)/shard_map/while/body/eval_jaxpr/reduce_sum | solution.py:45
  26.8 0.9 dynamic-slice_bitcast_fusion.11
  27.7 3.6 %fusion.49 = (f32[16,16,8]{2,1,0:T(8,128)S(1)}, f32[16,128]{1,0:T(8,128)S(1)}, f32[16,128]{1,0:T(8,128)S(1)}, f32[16,16,8]{2,1,0:T(8,128)S(1)}, f32[16,128]{1,0:...) fusion(f32[16,128]{1,0:T(8,128)S(1)} %get-tuple-element.434, ...), kind=kLoop, calls=%fused_computation.82.clone.1 | loop fusion | flops 11780096 | bytes 311296 | tf_op jit(solution)/shard_map/while/body/eval_jaxpr/reduce_sum | solution.py:45
  33.7 0.9 dynamic-slice_bitcast_fusion.11
  34.6 3.6 %fusion.49 = (f32[16,16,8]{2,1,0:T(8,128)S(1)}, f32[16,128]{1,0:T(8,128)S(1)}, f32[16,128]{1,0:T(8,128)S(1)}, f32[16,16,8]{2,1,0:T(8,128)S(1)}, f32[16,128]{1,0:...) fusion(f32[16,128]{1,0:T(8,128)S(1)} %get-tuple-element.434, ...), kind=kLoop, calls=%fused_computation.82.clone.1 | loop fusion | flops 11780096 | bytes 311296 | tf_op jit(solution)/shard_map/while/body/eval_jaxpr/reduce_sum | solution.py:45
  39.4 3.7 %collective-permute-start = (f32[8,1,7,128]{3,0,2,1:T(8,128)S(1)}, f32[8,1,7,128]{3,0,2,1:T(8,128)S(1)}, u32[]{:S(2)}, u32[]{:S(2)}) collective-permute-start(f32[8,1,7,128]{3,0,2,1:T(8,128)S(1)} %bitcast.256), channel_id=1, source_target_pairs={{0,24},{8,0},{16,8},{24,16},{1,25},{9,1},{17,9},{25,17},{2,26},{10... | collective-permute-start | bytes 86024 | tf_op jit(solution)/shard_map/ppermute | solution.py:16
  43.8 0.9 collective-permute-done
  44.7 4.1 %collective-permute-done.1 = f32[8,1,7,128]{3,0,2,1:T(8,128)S(1)} collective-permute-done((f32[8,1,7,128]{3,0,2,1:T(8,128)S(1)}, f32[8,1,7,128]{3,0,2,1:T(8,128)S(1)}, u32[]{:S(2)}, u32[]{:S(2)}) %collective-permute-start.1) | collective-permute-done | bytes 28704 | tf_op jit(solution)/shard_map/ppermute | solution.py:16
  48.8 20.6 %while.24 = (s32[]{:T(128)}, f32[3,16,4,128]{3,1,0,2:T(8,128)S(1)}, f32[3,16,4,128]{3,1,0,2:T(8,128)S(1)}, f32[3,16,7,128]{3,1,0,2:T(8,128)S(1)}, f32[3,16,7,128...) while((s32[]{:T(128)}, f32[3,16,4,128]{3,1,0,2:T(8,128)S(1)}, ...), condition=%wide.region_9.10_spmd, body=%wide.region_0.9_spmd.sunk | while | flops 11837442 | bytes 1654877 | solution.py:56
  50.0 0.9 dynamic-slice_bitcast_fusion.9
  50.9 3.6 %fusion.47 = (f32[16,16,8]{2,1,0:T(8,128)S(1)}, f32[16,128]{1,0:T(8,128)S(1)}, f32[16,128]{1,0:T(8,128)S(1)}, f32[16,16,8]{2,1,0:T(8,128)S(1)}, f32[16,128]{1,0:...) fusion(f32[16,128]{1,0:T(8,128)S(1)} %get-tuple-element.404, ...), kind=kLoop, calls=%fused_computation.34.clone.1 | loop fusion | flops 11780096 | bytes 311296 | tf_op jit(solution)/shard_map/while/body/eval_jaxpr/reduce_sum | solution.py:45
  56.9 0.9 dynamic-slice_bitcast_fusion.9
  57.8 3.6 %fusion.47 = (f32[16,16,8]{2,1,0:T(8,128)S(1)}, f32[16,128]{1,0:T(8,128)S(1)}, f32[16,128]{1,0:T(8,128)S(1)}, f32[16,16,8]{2,1,0:T(8,128)S(1)}, f32[16,128]{1,0:...) fusion(f32[16,128]{1,0:T(8,128)S(1)} %get-tuple-element.404, ...), kind=kLoop, calls=%fused_computation.34.clone.1 | loop fusion | flops 11780096 | bytes 311296 | tf_op jit(solution)/shard_map/while/body/eval_jaxpr/reduce_sum | solution.py:45
  63.7 0.9 dynamic-slice_bitcast_fusion.9
  64.6 3.6 %fusion.47 = (f32[16,16,8]{2,1,0:T(8,128)S(1)}, f32[16,128]{1,0:T(8,128)S(1)}, f32[16,128]{1,0:T(8,128)S(1)}, f32[16,16,8]{2,1,0:T(8,128)S(1)}, f32[16,128]{1,0:...) fusion(f32[16,128]{1,0:T(8,128)S(1)} %get-tuple-element.404, ...), kind=kLoop, calls=%fused_computation.34.clone.1 | loop fusion | flops 11780096 | bytes 311296 | tf_op jit(solution)/shard_map/while/body/eval_jaxpr/reduce_sum | solution.py:45
  69.6 3.8 %collective-permute-start.3 = (f32[8,1,4,128]{3,0,2,1:T(8,128)S(1)}, f32[8,1,4,128]{3,0,2,1:T(8,128)S(1)}, u32[]{:S(2)}, u32[]{:S(2)}) collective-permute-start(f32[8,1,4,128]{3,0,2,1:T(8,128)S(1)} %get-tuple-element.282), channel_id=1, source_target_pairs={{0,24},{8,0},{16,8},{24,16},{1,25},{9,1},{17,9},{25,17},{2,26},{10... | collective-permute-start | bytes 49160 | tf_op jit(solution)/shard_map/ppermute | solution.py:16
  73.4 1.7 %collective-permute-done.2 = f32[8,1,4,128]{3,0,2,1:T(8,128)S(1)} collective-permute-done((f32[8,1,4,128]{3,0,2,1:T(8,128)S(1)}, f32[8,1,4,128]{3,0,2,1:T(8,128)S(1)}, u32[]{:S(2)}, u32[]{:S(2)}) %collective-permute-start.2) | collective-permute-done | bytes 16416 | tf_op jit(solution)/shard_map/ppermute | solution.py:16
  75.8 4.2 %all-to-all-start.1 = ((f32[3,8,1,4,128]{4,3,0,2,1:T(4,128)}), f32[3,8,1,4,128]{4,3,0,2,1:T(4,128)S(1)}, u32[]{:S(2)}, u32[]{:S(2)}) async-start(f32[3,8,1,4,128]{4,3,0,2,1:T(4,128)} %copy.387), calls=%async_computation.1 | async-start | bytes 98304 | tf_op jit(solution)/shard_map/all_to_all | solution.py:115
  80.3 2.2 %scatter_fusion = f32[64,4,128]{2,1,0:T(4,128)S(1)} fusion(f32[64,4,128]{2,1,0:T(4,128)S(1)} %broadcast_in_dim.56, s32[48]{0:T(128)S(1)} %fusion.37, f32[48,4,128]{2,1,0:T(4,128)S(1)} %copy.378), kind=kCustom, calls=%fused_computation.5 | custom fusion | flops 24576 | bytes 295104 | tf_op jit(solution)/shard_map/scatter-add | solution.py:102
  82.5 2.7 %scatter_fusion.1 = f32[64,4,128]{2,1,0:T(4,128)S(1)} fusion(f32[64,4,128]{2,1,0:T(4,128)S(1)} %scatter_fusion, s32[64]{0:T(128)S(1)} %get-tuple-element.285, f32[64,4,128]{2,1,0:T(4,128)S(1)} %copy.383), kind=kCustom, calls=%fused_computation.6 | custom fusion | flops 32768 | bytes 393472 | tf_op jit(solution)/shard_map/scatter-add | solution.py:112
  85.3 2.8 %scatter_fusion.2 = f32[64,4,128]{2,1,0:T(4,128)S(1)} fusion(f32[64,4,128]{2,1,0:T(4,128)S(1)} %scatter_fusion.1, s32[64]{0:T(128)S(1)} %get-tuple-element.284, f32[64,4,128]{2,1,0:T(4,128)S(1)} %copy.385), kind=kCustom, calls=%fused_computation.7 | custom fusion | flops 32768 | bytes 393472 | tf_op jit(solution)/shard_map/scatter-add | solution.py:112
  88.1 1.7 %scatter_fusion.3 = f32[64,4,128]{2,1,0:T(4,128)S(1)} fusion(f32[64,4,128]{2,1,0:T(4,128)S(1)} %scatter_fusion.2, s32[24]{0:T(128)S(1)} %fusion.38, f32[24,4,128]{2,1,0:T(4,128)S(1)} %copy.389), kind=kCustom, calls=%fused_computation.8 | custom fusion | flops 12288 | bytes 147552 | tf_op jit(solution)/shard_map/scatter-add | solution.py:116
  92.6 4.2 %all-to-all-start.2 = ((f32[8,1,11,128]{3,1,2,0:T(1,128)}), f32[8,1,11,128]{3,1,2,0:T(1,128)S(1)}, u32[]{:S(2)}, u32[]{:S(2)}) async-start(f32[8,1,11,128]{3,1,2,0:T(1,128)} %copy.395), calls=%async_computation.2 | async-start | bytes 90112 | tf_op jit(solution)/shard_map/all_to_all | solution.py:127
  96.8 0.7 pad_maximum_fusion.1
  98.2 3.5 %all-to-all-done.2 = f32[8,1,11,128]{3,1,2,0:T(1,128)S(1)} async-done(((f32[8,1,11,128]{3,1,2,0:T(1,128)}), f32[8,1,11,128]{3,1,2,0:T(1,128)S(1)}, u32[]{:S(2)}, u32[]{:S(2)}) %all-to-all-start.2) | async-done | bytes 45088 | tf_op jit(solution)/shard_map/all_to_all | solution.py:127
  (272 shorter events, 25.0 us)
Async XLA Ops:
  0.6 1.8 %copy-start = (f32[64,4,128]{2,1,0:T(4,128)S(1)}, f32[64,4,128]{2,1,0:T(4,128)}, u32[]{:S(2)}) copy-start(f32[64,4,128]{2,1,0:T(4,128)} %param.15) | copy-start | bytes 393220
  1.6 0.7 copy-start.3
  3.8 35.6 %all-to-all-start = ((f32[3,8,1,7,128]{4,2,3,0,1:T(1,128)}), f32[3,8,1,7,128]{4,2,3,0,1:T(1,128)S(1)}, u32[]{:S(2)}, u32[]{:S(2)}) async-start(f32[3,8,1,7,128]{4,2,3,0,1:T(1,128)} %copy.371), calls=%async_computation | async-start | bytes 172032 | tf_op jit(solution)/shard_map/all_to_all | solution.py:85
  9.0 0.7 copy-start.5
  9.9 0.7 copy-start.4
  11.9 27.5 %copy-start.6 = (s32[1,8,1]{1,2,0:T(1,128)S(1)}, s32[1,8,1]{1,2,0:T(1,128)}, u32[]{:S(2)}) copy-start(s32[1,8,1]{1,2,0:T(1,128)} %param.23) | copy-start | bytes 100
  39.4 5.2 %collective-permute-start = (f32[8,1,7,128]{3,0,2,1:T(8,128)S(1)}, f32[8,1,7,128]{3,0,2,1:T(8,128)S(1)}, u32[]{:S(2)}, u32[]{:S(2)}) collective-permute-start(f32[8,1,7,128]{3,0,2,1:T(8,128)S(1)} %bitcast.256), channel_id=1, source_target_pairs={{0,24},{8,0},{16,8},{24,16},{1,25},{9,1},{17,9},{25,17},{2,26},{10... | collective-permute-start | bytes 86024 | tf_op jit(solution)/shard_map/ppermute | solution.py:16
  43.1 5.7 %collective-permute-start.1 = (f32[8,1,7,128]{3,0,2,1:T(8,128)S(1)}, f32[8,1,7,128]{3,0,2,1:T(8,128)S(1)}, u32[]{:S(2)}, u32[]{:S(2)}) collective-permute-start(f32[8,1,7,128]{3,0,2,1:T(8,128)S(1)} %bitcast.257), channel_id=1, source_target_pairs={{0,8},{8,16},{16,24},{24,0},{1,9},{9,17},{17,25},{25,1},{2,10},{10... | collective-permute-start | bytes 86024 | tf_op jit(solution)/shard_map/ppermute | solution.py:16
  69.6 5.6 %collective-permute-start.2 = (f32[8,1,4,128]{3,0,2,1:T(8,128)S(1)}, f32[8,1,4,128]{3,0,2,1:T(8,128)S(1)}, u32[]{:S(2)}, u32[]{:S(2)}) collective-permute-start(f32[8,1,4,128]{3,0,2,1:T(8,128)S(1)} %get-tuple-element.281), channel_id=1, source_target_pairs={{0,8},{8,16},{16,24},{24,0},{1,9},{9,17},{17,25},{25,1},{2,10},{10... | collective-permute-start | bytes 49160 | tf_op jit(solution)/shard_map/ppermute | solution.py:16
  69.6 5.5 %collective-permute-start.3 = (f32[8,1,4,128]{3,0,2,1:T(8,128)S(1)}, f32[8,1,4,128]{3,0,2,1:T(8,128)S(1)}, u32[]{:S(2)}, u32[]{:S(2)}) collective-permute-start(f32[8,1,4,128]{3,0,2,1:T(8,128)S(1)} %get-tuple-element.282), channel_id=1, source_target_pairs={{0,24},{8,0},{16,8},{24,16},{1,25},{9,1},{17,9},{25,17},{2,26},{10... | collective-permute-start | bytes 49160 | tf_op jit(solution)/shard_map/ppermute | solution.py:16
  75.8 12.2 %all-to-all-start.1 = ((f32[3,8,1,4,128]{4,3,0,2,1:T(4,128)}), f32[3,8,1,4,128]{4,3,0,2,1:T(4,128)S(1)}, u32[]{:S(2)}, u32[]{:S(2)}) async-start(f32[3,8,1,4,128]{4,3,0,2,1:T(4,128)} %copy.387), calls=%async_computation.1 | async-start | bytes 98304 | tf_op jit(solution)/shard_map/all_to_all | solution.py:115
  88.1 1.8 %copy-start.2 = (f32[64,3,128]{2,0,1:T(8,128)S(1)}, f32[64,3,128]{2,0,1:T(8,128)}, u32[]{:S(2)}) copy-start(f32[64,3,128]{2,0,1:T(8,128)} %param.17) | copy-start | bytes 294916
  89.9 0.8 copy-start.1
  92.6 9.1 %all-to-all-start.2 = ((f32[8,1,11,128]{3,1,2,0:T(1,128)}), f32[8,1,11,128]{3,1,2,0:T(1,128)S(1)}, u32[]{:S(2)}, u32[]{:S(2)}) async-start(f32[8,1,11,128]{3,1,2,0:T(1,128)} %copy.395), calls=%async_computation.2 | async-start | bytes 90112 | tf_op jit(solution)/shard_map/all_to_all | solution.py:127
where the time goes:
time: 103 us; the launch traced here: 102 us
  other arithmetic  36.8 us (36%)
  local copies, waits for them, and re-layouts  31.9 us (31%)
  starting transfers between devices  21.1 us (20%)
  waiting for transfers between devices  10.2 us (10%)
  loops' own time  1.35 us (1%)
    reduce_sum x7, other arithmetic, tile_group(): on_others = jnp.stack([-jnp.sum(t, axis=2) for t in terms], axis=1)  25.4 us
    ppermute x4, starting transfers between devices, from_behind(): lax.ppermute(shard, axis, [(i, (i + by) % peers) for i in range(peers)])  7.53 us
    ppermute x4, waiting for transfers between devices, from_behind(): lax.ppermute(shard, axis, [(i, (i + by) % peers) for i in range(peers)])  6.68 us
    shift_right_arithmetic x7, local copies, waits for them, and re-layouts, unpack_bonds(): jnp.right_shift(packed[:, :, None, :], shifts[None, None, :, None])  6.44 us
    scatter-add x2, other arithmetic, per_device(): totals.at[first_block].add(pair_first).at[second_block].add(pair_second)  5.5 us
    all_to_all x1, starting transfers between devices, per_device(): lax.all_to_all(outgoing, 'bulk', split_axis=1, concat_axis=1, tiled=True)  5.17 us
    unnamed x20, local copies, waits for them, and re-layouts  4.41 us
    all_to_all x1, starting transfers between devices, per_device(): lax.all_to_all(chosen, 'bulk', split_axis=0, concat_axis=0, tiled=True)  4.2 us
  transfers between devices with their start and end apart: 7, of which 4 were waited for; matrix products, arithmetic and copies ran while one was open for 37% of the time, Pallas kernels for 0%

commit v1 on v0

v1 whole, which is shorter than its diff:
```python
import functools

import jax
import jax.numpy as jnp
from jax import lax
from jax.experimental import pallas as pl
from jax.experimental.pallas import tpu as pltpu
from jax.sharding import PartitionSpec as P

MESH = pl.DeviceIdType.MESH
bond_stiff = 0.1
leak_gain = 0.5
time_step = 0.5
half_press = 0.025
F32 = jnp.float32
BF16 = jnp.bfloat16


def rows_of(shape):
    return lax.broadcasted_iota(jnp.int32, shape, len(shape) - 2)


def roll(x, by):
    return pltpu.roll(x, by % 8, x.ndim - 2)


def top(x):
    return x.astype(BF16).astype(F32)


def split3(x):
    first = top(x)
    rest = x - first
    second = top(rest)
    return first, second, rest - second


def features(block):
    row = rows_of(block.shape)
    half = jnp.where(row < 3, 0.5 * block, 0.0)
    norm = jnp.sum(half * half, axis=-2, keepdims=True) + 0.5
    as_b = jnp.where(row == 3, norm, jnp.where(row == 4, 1.0, half))
    as_a = jnp.where(row == 3, 1.0, jnp.where(row == 4, norm, -2.0 * half))
    b1, b2, b3 = split3(as_b)
    a1, a2, a3 = split3(as_a)
    left = jnp.concatenate([b1, b1, b2, b2, b1, b3], axis=-2).astype(BF16)
    right = jnp.concatenate([a1, a2, a1, a2, a3, a1], axis=-2).astype(BF16)
    press = block[..., 6:7, :]
    moved = roll(block, -3)
    product = -0.25 * press * block
    product_top = top(product)
    moved_top = top(moved)
    block_top = top(block)
    press_top = top(press)
    spring_0 = jnp.where(row < 3, moved_top, jnp.where(row == 3, 1.0, 0.0))
    spring_1 = jnp.where((row >= 1) & (row < 4), roll(moved - moved_top, 1), 0.0)
    leak_0 = jnp.where(
        row < 3,
        product_top,
        jnp.where(
            row == 3, 0.0, jnp.where(row == 4, 1.0, jnp.where(row == 5, press_top, roll(block_top, 6)))
        ),
    )
    leak_1 = jnp.where(
        row == 0,
        roll(block_top, 6),
        jnp.where(
            row < 4,
            roll(product - product_top, 1),
            jnp.where(row == 4, press - press_top, roll(block - block_top, 5)),
        ),
    )
    sums = jnp.concatenate(
        [
            jnp.concatenate([spring_0, spring_1], axis=-2),
            jnp.concatenate([leak_0, leak_1], axis=-2),
        ],
        axis=-1,
    ).astype(BF16)
    return left, right, sums


def combine(block, out):
    row = rows_of(block.shape)
    r0, r1 = out[:8], out[8:]
    o1 = r0 + roll(r1, -1)
    o2 = r0[3:4]
    o4 = r0[4:5]
    o5 = r0[5:6] + r1[4:5]
    o3 = jnp.where(row < 2, roll(r0, 2), roll(r1, 2)) + roll(r1, 3)
    press = block[6:7]
    force = bond_stiff * (o1 - roll(block, -3) * o2) + half_press * (
        block * (press * o4 + o5) - press * o3
    )
    leak = leak_gain * (o5 - press * o4)
    return jnp.where(row < 3, force, jnp.where(row == 3, leak, 0.0))


def tile(left_b, right_a, sums_b, sums_a, packed):
    dist = lax.dot_general(
        left_b, right_a, (((0,), (0,)), ((), ())), preferred_element_type=F32
    )
    guess = pl.reciprocal(dist, approx=True)
    weight = guess * (2.0 - dist * guess)
    words, width = packed.shape
    bit = lax.shift_left(1, rows_of((1, 8, width)))
    intact = (jnp.broadcast_to(packed[:, None, :], (words, 8, width)) & bit) != 0
    intact = intact.reshape(words * 8, width)
    spring = jnp.where(intact, weight, 0.0)
    leak = jnp.where(intact, 0.0, weight)
    spring_hi = spring.astype(BF16)
    leak_hi = leak.astype(BF16)
    spring_lo = (spring - spring_hi.astype(F32)).astype(BF16)
    leak_lo = (leak - leak_hi.astype(F32)).astype(BF16)
    along_j = (((1,), (0,)), ((), ()))
    along_i = (((1,), (1,)), ((), ()))
    dot = functools.partial(lax.dot_general, preferred_element_type=F32)
    on_a = dot(sums_b, jnp.concatenate([spring_hi, leak_hi], axis=0), along_j) + dot(
        sums_b, jnp.concatenate([spring_lo, leak_lo], axis=0), along_j
    )
    on_b = dot(sums_a, jnp.concatenate([spring_hi, leak_hi], axis=1), along_i) + dot(
        sums_a, jnp.concatenate([spring_lo, leak_lo], axis=1), along_i
    )
    return on_a, on_b


def kernel(
    nreg,
    nbulk,
    pos_ref,
    fld_ref,
    sto_ref,
    vel_ref,
    send_s,
    touch_s,
    pair_s,
    move_s,
    send_v,
    touch_v,
    pair_v,
    rmask_ref,
    lmask_ref,
    nf_ref,
    nv_ref,
    arr_ref,
    pts,
    stage,
    got,
    back,
    ret,
    mstage,
    mgot,
    left,
    right,
    sums,
    terms,
    send1,
    recv1,
    send2,
    recv2,
    send3,
    recv3,
):
    blocks, width = sto_ref.shape
    slots = send_s.shape[1]
    per = nbulk * slots
    recv_count = 3 * per
    pairs = pair_s.shape[1]
    touch = touch_s.shape[0]
    mig = move_s.shape[0]
    r = lax.axis_index("region")
    me = lax.axis_index("bulk")

    def region_at(by):
        return lax.rem(r + by + nreg, nreg)

    peers = []
    for o in (0, 2, 1):
        for step in range(nbulk):
            if o == 1 and step == 0:
                continue
            peers.append((o, lax.rem(me + step, nbulk)))

    barrier = pltpu.get_barrier_semaphore()
    for o, d in peers:
        pl.semaphore_signal(barrier, inc=1, device_id=(region_at(o - 1), d), device_id_type=MESH)

    for k in range(3):
        pts[:, k, :] = pos_ref[k]
    for k in range(4):
        pts[:, 3 + k, :] = fld_ref[:, k, :]
    pts[:, 7, :] = jnp.zeros((blocks, width), F32)
    for o in range(3):
        for s in range(slots):
            for d in range(nbulk):
                stage[o, d * slots + s] = pts[send_s[o, s, d]]
    for s in range(slots):
        got[1, me * slots + s] = stage[1, me * slots + s]

    def span(ref, o, d):
        return ref.at[o, pl.ds(d * slots, slots)]

    def copy1(o, d):
        return pltpu.make_async_remote_copy(
            src_ref=span(stage, o, d),
            dst_ref=span(got, o, me),
            send_sem=send1.at[o, d],
            recv_sem=recv1.at[o, me],
            device_id=(region_at(o - 1), d),
            device_id_type=MESH,
        )

    def copy2(o, b):
        return pltpu.make_async_remote_copy(
            src_ref=span(back, o, b),
            dst_ref=span(ret, o, me),
            send_sem=send2.at[o, b],
            recv_sem=recv2.at[o, me],
            device_id=(region_at(1 - o), b),
            device_id_type=MESH,
        )

    def copy3(d):
        return pltpu.make_async_remote_copy(
            src_ref=mstage.at[pl.ds(d * mig, mig)],
            dst_ref=mgot.at[pl.ds(me * mig, mig)],
            send_sem=send3.at[d],
            recv_sem=recv3.at[me],
            device_id=(r, d),
            device_id_type=MESH,
        )

    def arrival(ref, sem, o, b):
        pltpu.make_async_copy(span(ref, o, b), span(ref, o, b), sem.at[o, b]).wait()

    pl.semaphore_wait(barrier, len(peers))
    for o, d in peers:
        copy1(o, d).start()

    group = 8

    def build(step, carry):
        at = pl.ds(step * group, group)
        left[at], right[at], sums[at] = features(pts[at])
        return carry

    lax.fori_loop(0, blocks // group, build, 0)
    base = 2 * pairs
    used = base + touch * recv_count + recv_count
    rows = terms.shape[1]
    terms[:, base:, :] = jnp.zeros((4, rows - base, width), F32)

    def put(t, value):
        terms[:, pl.ds(t, 1), :] = value[0:4].reshape(4, 1, width)

    def local(t):
        a = pair_s[0, t]
        b = pair_s[1, t]
        on_a, on_b = tile(left[b], right[a], sums[b], sums[a], lmask_ref[t])
        put(t, combine(pts[a], on_a))
        put(pairs + t, combine(pts[b], on_b))

    def locals_(step, carry):
        local(2 * step)
        local(2 * step + 1)
        return carry

    lax.fori_loop(0, pairs // 2, locals_, 0)

    def remote(q, carry):
        o = q // per
        b = lax.rem(q, per) // slots
        s = lax.rem(q, slots)
        own = (o == 1) & (b == me)

        if slots == 1:
            @pl.when(jnp.logical_not(own))
            def _():
                arrival(got, recv1, o, b)
        else:
            @pl.when(jnp.logical_not(own) & (s == 0))
            def _():
                arrival(got, recv1, o, b)

        block = got[o, lax.rem(q, per)]
        left_b, _, sums_b = features(block[None])
        total = None
        for t in range(touch):
            a = touch_s[t, q]
            on_a, on_b = tile(left_b[0], right[a], sums_b[0], sums[a], rmask_ref[q, t])
            put(base + t * recv_count + q, combine(pts[a], on_a))
            total = on_b if total is None else total + on_b
        back[o, lax.rem(q, per)] = combine(block, total)

        @pl.when(jnp.logical_not(own) & (s == slots - 1))
        def _():
            copy2(o, b).start()

        return carry

    lax.fori_loop(0, recv_count, remote, 0)
    for s in range(slots):
        ret[1, me * slots + s] = back[1, me * slots + s]
    for o, d in peers:
        arrival(ret, recv2, o, d)
    for o in range(3):
        for d in range(per):
            put(base + touch * recv_count + o * per + d, ret[o, d])

    index = jnp.concatenate(
        [pair_v[0:1], pair_v[1:2]]
        + [touch_v[t : t + 1] for t in range(touch)]
        + [send_v[o] for o in range(3)]
        + [jnp.full((1, rows - used), -1, jnp.int32)],
        axis=1,
    )
    here = lax.broadcasted_iota(jnp.int32, (blocks, rows), 0)
    pick = jnp.where(here == index, 1.0, 0.0).astype(BF16)
    totals = []
    for k in range(4):
        parts = split3(terms[k])
        totals.append(
            sum(jnp.dot(pick, part.astype(BF16), preferred_element_type=F32) for part in parts)
        )
    for k in range(3):
        speed = vel_ref[k] + time_step * totals[k]
        nv_ref[k] = speed
        nf_ref[:, k, :] = fld_ref[:, k, :] + time_step * speed
    nf_ref[:, 3, :] = fld_ref[:, 3, :] + time_step * totals[3] / sto_ref[...]

    for d in range(nbulk):
        for m in range(mig):
            entry = move_s[m, 0, d]
            at = jnp.maximum(entry, 0)
            live = entry >= 0
            slot = d * mig + m
            mstage[slot, 0:4] = jnp.where(live, nf_ref[at], 0.0)
            for k in range(3):
                mstage[slot, 4 + k : 5 + k] = jnp.where(live, nv_ref[k, pl.ds(at, 1), :], 0.0)
                mstage[slot, 7 + k : 8 + k] = jnp.where(live, pos_ref[k, pl.ds(at, 1), :], 0.0)
            mstage[slot, 10:11] = jnp.where(live, sto_ref[pl.ds(at, 1), :], 0.0)
            mstage[slot, 11:16] = jnp.zeros((5, width), F32)
    others = [lax.rem(me + step, nbulk) for step in range(1, nbulk)]
    for d in others:
        copy3(d).start()
    for m in range(mig):
        mgot[me * mig + m] = mstage[me * mig + m]
    for o, d in peers:
        copy1(o, d).wait_send()
        copy2(o, d).wait_send()
    for d in others:
        landed = mgot.at[pl.ds(d * mig, mig)]
        pltpu.make_async_copy(landed, landed, recv3.at[d]).wait()
    for k in range(11):
        arr_ref[k] = mgot[:, k, :]
    for d in others:
        copy3(d).wait_send()


def solution(mesh):
    nreg, nbulk = mesh.shape["region"], mesh.shape["bulk"]

    def per_device(
        positions,
        fields,
        storage,
        velocity,
        send_list,
        remote_local,
        remote_mask,
        local_pairs,
        local_mask,
        migrate_list,
    ):
        blocks, _, width = positions.shape
        slots = send_list.shape[3]
        recv_count, touch = remote_local.shape[1:]
        pairs = local_pairs.shape[1]
        mig = migrate_list.shape[2]
        per = nbulk * slots
        rows = -(-(2 * pairs + (touch + 1) * recv_count) // 128) * 128
        sends = send_list[0].transpose(0, 2, 1)
        touches = remote_local[0].T
        pair_rows = local_pairs[0].T
        moves = migrate_list[0].T[:, None, :]
        vmem = pl.BlockSpec(memory_space=pltpu.VMEM)
        smem = pl.BlockSpec(memory_space=pltpu.SMEM)
        dma = pltpu.SemaphoreType.DMA
        new_fields, speed, arrived = pl.pallas_call(
            functools.partial(kernel, nreg, nbulk),
            out_shape=(
                jax.ShapeDtypeStruct((blocks, 4, width), F32),
                jax.ShapeDtypeStruct((3, blocks, width), F32),
                jax.ShapeDtypeStruct((11, nbulk * mig, width), F32),
            ),
            in_specs=[vmem] * 4 + [smem] * 4 + [vmem] * 5,
            out_specs=(vmem, vmem, vmem),
            scratch_shapes=[
                pltpu.VMEM((blocks, 8, width), F32),
                pltpu.VMEM((3, per, 8, width), F32),
                pltpu.VMEM((3, per, 8, width), F32),
                pltpu.VMEM((3, per, 8, width), F32),
                pltpu.VMEM((3, per, 8, width), F32),
                pltpu.VMEM((nbulk * mig, 16, width), F32),
                pltpu.VMEM((nbulk * mig, 16, width), F32),
                pltpu.VMEM((blocks, 48, width), BF16),
                pltpu.VMEM((blocks, 48, width), BF16),
                pltpu.VMEM((blocks, 16, 2 * width), BF16),
                pltpu.VMEM((4, rows, width), F32),
                dma((3, nbulk)),
                dma((3, nbulk)),
                dma((3, nbulk)),
                dma((3, nbulk)),
                dma((nbulk,)),
                dma((nbulk,)),
            ],
            compiler_params=pltpu.CompilerParams(
                collective_id=0, has_side_effects=True, vmem_limit_bytes=32 << 20
            ),
        )(
            positions.transpose(1, 0, 2),
            fields,
            storage,
            velocity.transpose(1, 0, 2),
            sends,
            touches,
            pair_rows,
            moves,
            sends,
            touches,
            pair_rows,
            remote_mask[0],
            local_mask[0],
        )
        return new_fields, speed.transpose(1, 0, 2), arrived.transpose(1, 0, 2)

    both = ("region", "bulk")
    return jax.shard_map(
        per_device,
        mesh=mesh,
        in_specs=(
            P(both, None, None),
            P(both, None, None),
            P(both, None),
            P(both, None, None),
            P(both, None, None, None),
            P(both, None, None),
            P(both, None, None, None, None),
            P(both, None, None),
            P(both, None, None, None),
            P(both, None, None),
        ),
        out_specs=(
            P(both, None, None),
            P(both, None, None),
            P(both, None, None),
        ),
        check_vma=False,
    )
```

time: 103 us -> 56.5 us (0.55)
  Pallas kernels: 0 us -> 47.3 us
  other arithmetic: 36.8 us -> 0 us
  local copies, waits for them, and re-layouts: 31.9 us -> 8.09 us
  starting transfers between devices: 21.1 us -> 0 us
  waiting for transfers between devices: 10.2 us -> 0 us
  loops' own time: 1.35 us -> 0 us
    pallas_call x0 -> x1, Pallas kernels: none -> 47.3 us  [per_device(): pl.pallas_call(functools.partial(kernel, nreg, nbulk), out_shape=(jax.Sha...]
    reduce_sum x8 -> x0, other arithmetic: 25.5 us -> none  [the longest x7 25.4 us: tile_group(): on_others = jnp.stack([-jnp.sum(t, axis=2) for t in terms], axis=1)]
    all_to_all x3 -> x0, starting transfers between devices: 13.6 us -> none  [the longest x1 5.17 us: per_device(): lax.all_to_all(outgoing, 'bulk', split_axis=1, concat_axis=1, tiled=True)]
    scatter-add x4 -> x0, other arithmetic: 9.4 us -> none  [the longest x2 5.5 us: per_device(): totals.at[first_block].add(pair_first).at[second_block].add(pair_second)]
    ppermute x4 -> x0, starting transfers between devices: 7.53 us -> none  [from_behind(): lax.ppermute(shard, axis, [(i, (i + by) % peers) for i in range(peers)])]
    ppermute x4 -> x0, waiting for transfers between devices: 6.68 us -> none  [from_behind(): lax.ppermute(shard, axis, [(i, (i + by) % peers) for i in range(peers)])]
    shift_right_arithmetic x7 -> x0, local copies, waits for them, and re-layouts: 6.44 us -> none  [unpack_bonds(): jnp.right_shift(packed[:, :, None, :], shifts[None, None, :, None])]
    sub x56 -> x0, local copies, waits for them, and re-layouts: 4.99 us -> none  [the longest x35 2.64 us: tile_group(): others[:, 3 + k, :, None] - owned[:, 3 + k, None, :]]
  transfers between devices with their start and end apart: 7 -> 0, of which waited for: 4 -> 0; matrix products, arithmetic and copies ran while one was open for 37% -> 0% of each run, Pallas kernels for 0% -> 0%
where the time goes in v1:
time: 56.5 us; the launch traced here: 56.1 us
  Pallas kernels  47.3 us (84%)
  local copies, waits for them, and re-layouts  8.09 us (14%)
  between operations  0.68 us (1%)
    pallas_call x1, Pallas kernels, per_device(): pl.pallas_call(functools.partial(kernel, nreg, nbulk), out_shape=(jax.Sha...  47.3 us
    unnamed x23, local copies, waits for them, and re-layouts  8.09 us

profile of v1, /device:TPU:0, one launch (start us, length us, event | category | flops | bytes accessed | tf_op | source)
XLA Modules:
  0.0 56.1 jit_solution(3508041025052943204)
XLA Ops:
  0.6 0.0 copy-start.9
  0.6 0.0 copy-start.6
  0.7 0.0 copy-start.8
  0.7 0.0 copy-start.7
  0.7 0.6 %copy-done.9 = s32[1,8,1]{1,2,0:T(1,128)S(1)} copy-done((s32[1,8,1]{1,2,0:T(1,128)S(1)}, s32[1,8,1]{1,2,0:T(1,128)}, u32[]{:S(2)}) %copy-start.9) | copy-done | bytes 56
  1.3 0.0 copy-done.6
  1.3 0.0 copy-done.8
  1.3 0.0 copy-done.7
  1.4 0.0 copy-start
  1.4 1.0 %copy-done = s32[1,64,16,128]{3,2,1,0:T(8,128)S(1)} copy-done((s32[1,64,16,128]{3,2,1,0:T(8,128)S(1)}, s32[1,64,16,128]{3,2,1,0:T(8,128)}, u32[]{:S(2)}) %copy-start) | copy-done | bytes 524312
  2.4 0.0 copy-start.1
  2.4 1.0 %copy-done.1 = s32[1,24,2,16,128]{4,3,2,1,0:T(8,128)S(1)} copy-done((s32[1,24,2,16,128]{4,3,2,1,0:T(8,128)S(1)}, s32[1,24,2,16,128]{4,3,2,1,0:T(8,128)}, u32[]{:S(2)}) %copy-start.1) | copy-done | bytes 393240
  3.4 0.0 copy-start.2
  3.4 0.9 %copy-done.2 = f32[64,4,128]{2,1,0:T(4,128)S(1)} copy-done((f32[64,4,128]{2,1,0:T(4,128)S(1)}, f32[64,4,128]{2,1,0:T(4,128)}, u32[]{:S(2)}) %copy-start.2) | copy-done | bytes 131096
  4.3 0.0 copy-start.3
  4.3 0.9 %copy-done.3 = f32[64,3,128]{2,0,1:T(8,128)S(1)} copy-done((f32[64,3,128]{2,0,1:T(8,128)S(1)}, f32[64,3,128]{2,0,1:T(8,128)}, u32[]{:S(2)}) %copy-start.3) | copy-done | bytes 98328
  5.2 0.0 copy-start.4
  5.2 0.9 %copy-done.4 = f32[64,3,128]{2,0,1:T(8,128)S(1)} copy-done((f32[64,3,128]{2,0,1:T(8,128)S(1)}, f32[64,3,128]{2,0,1:T(8,128)}, u32[]{:S(2)}) %copy-start.4) | copy-done | bytes 98328
  6.1 0.0 copy-start.5
  6.1 0.8 %copy-done.5 = f32[64,128]{1,0:T(8,128)S(1)} copy-done((f32[64,128]{1,0:T(8,128)S(1)}, f32[64,128]{1,0:T(8,128)}, u32[]{:S(2)}) %copy-start.5) | copy-done | bytes 32792
  6.8 47.3 %shard_map.121 = (f32[64,4,128]{2,1,0:T(4,128)S(1)}, f32[3,64,128]{2,1,0:T(8,128)S(1)}, f32[11,8,128]{2,1,0:T(8,128)S(1)}) custom-call(f32[3,64,128]{2,1,0:T(8,128)S(1)} %bitcast.17, f32[64,4,128]{2,1,0:T(4,128)S(1)} %copy-done.2, f32[64,128]{1,0:T(8,128)S(1)} %copy-done.5, f32[3,64,128]{2,1,0:T(8,128)S(1)} %bitcast.18, s32[3,1,8]{2,1,0:T(1,128)S(1)} %bitcast.20, ...), custom_call_target="tpu_custom_call" | custom-call | tf_op jit(solution)/shard_map/pallas_call | solution.py:389
  54.2 0.7 %copy.16 = f32[64,4,128]{2,1,0:T(4,128)} copy(f32[64,4,128]{2,1,0:T(4,128)S(1)} %get-tuple-element.12) | data formatting | bytes 262144
  54.8 0.6 %copy.17 = f32[64,3,128]{2,0,1:T(8,128)} copy(f32[64,3,128]{2,0,1:T(8,128)S(1)} %bitcast.16) | data formatting | bytes 196608
  55.5 0.6 %copy.18 = f32[8,11,128]{2,0,1:T(8,128)} copy(f32[8,11,128]{2,0,1:T(8,128)S(1)} %bitcast.19) | data formatting | bytes 90112
Async XLA Ops:
  0.6 0.7 %copy-start.9 = (s32[1,8,1]{1,2,0:T(1,128)S(1)}, s32[1,8,1]{1,2,0:T(1,128)}, u32[]{:S(2)}) copy-start(s32[1,8,1]{1,2,0:T(1,128)} %param.19) | copy-start | bytes 100
  0.6 0.7 %copy-start.6 = (s32[1,3,8,1]{2,3,1,0:T(1,128)S(1)}, s32[1,3,8,1]{2,3,1,0:T(1,128)}, u32[]{:S(2)}) copy-start(s32[1,3,8,1]{2,3,1,0:T(1,128)} %param.14) | copy-start | bytes 292
  0.7 0.7 %copy-start.8 = (s32[1,64,2]{1,2,0:T(2,128)S(1)}, s32[1,64,2]{1,2,0:T(2,128)}, u32[]{:S(2)}) copy-start(s32[1,64,2]{1,2,0:T(2,128)} %param.17) | copy-start | bytes 1540
  0.7 0.7 %copy-start.7 = (s32[1,24,2]{1,2,0:T(2,128)S(1)}, s32[1,24,2]{1,2,0:T(2,128)}, u32[]{:S(2)}) copy-start(s32[1,24,2]{1,2,0:T(2,128)} %param.15) | copy-start | bytes 580
  1.4 1.0 %copy-start = (s32[1,64,16,128]{3,2,1,0:T(8,128)S(1)}, s32[1,64,16,128]{3,2,1,0:T(8,128)}, u32[]{:S(2)}) copy-start(s32[1,64,16,128]{3,2,1,0:T(8,128)} %param.18) | copy-start | bytes 1572868
  2.4 1.0 %copy-start.1 = (s32[1,24,2,16,128]{4,3,2,1,0:T(8,128)S(1)}, s32[1,24,2,16,128]{4,3,2,1,0:T(8,128)}, u32[]{:S(2)}) copy-start(s32[1,24,2,16,128]{4,3,2,1,0:T(8,128)} %param.16) | copy-start | bytes 1179652
  3.4 0.9 %copy-start.2 = (f32[64,4,128]{2,1,0:T(4,128)S(1)}, f32[64,4,128]{2,1,0:T(4,128)}, u32[]{:S(2)}) copy-start(f32[64,4,128]{2,1,0:T(4,128)} %fld_ref.1) | copy-start | bytes 393220
  4.3 0.9 %copy-start.3 = (f32[64,3,128]{2,0,1:T(8,128)S(1)}, f32[64,3,128]{2,0,1:T(8,128)}, u32[]{:S(2)}) copy-start(f32[64,3,128]{2,0,1:T(8,128)} %param.10) | copy-start | bytes 294916
  5.2 0.9 %copy-start.4 = (f32[64,3,128]{2,0,1:T(8,128)S(1)}, f32[64,3,128]{2,0,1:T(8,128)}, u32[]{:S(2)}) copy-start(f32[64,3,128]{2,0,1:T(8,128)} %param.13) | copy-start | bytes 294916
  6.1 0.8 %copy-start.5 = (f32[64,128]{1,0:T(8,128)S(1)}, f32[64,128]{1,0:T(8,128)}, u32[]{:S(2)}) copy-start(f32[64,128]{1,0:T(8,128)} %sto_ref.1) | copy-start | bytes 98308

commit v2 on v1

--- a/solution.py
+++ b/solution.py
@@ -96,10 +96,16 @@
     return jnp.where(row < 3, force, jnp.where(row == 3, leak, 0.0))
 
 
-def tile(left_b, right_a, sums_b, sums_a, packed):
-    dist = lax.dot_general(
-        left_b, right_a, (((0,), (0,)), ((), ())), preferred_element_type=F32
-    )
+ALONG_J = (((1,), (0,)), ((), ()))
+ALONG_I = (((1,), (1,)), ((), ()))
+dot = functools.partial(lax.dot_general, preferred_element_type=F32)
+
+
+def distance(left_b, right_a):
+    return dot(left_b, right_a, (((0,), (0,)), ((), ())))
+
+
+def split_weights(dist, packed):
     guess = pl.reciprocal(dist, approx=True)
     weight = guess * (2.0 - dist * guess)
     words, width = packed.shape
@@ -112,21 +118,25 @@
     leak_hi = leak.astype(BF16)
     spring_lo = (spring - spring_hi.astype(F32)).astype(BF16)
     leak_lo = (leak - leak_hi.astype(F32)).astype(BF16)
-    along_j = (((1,), (0,)), ((), ()))
-    along_i = (((1,), (1,)), ((), ()))
-    dot = functools.partial(lax.dot_general, preferred_element_type=F32)
-    on_a = dot(sums_b, jnp.concatenate([spring_hi, leak_hi], axis=0), along_j) + dot(
-        sums_b, jnp.concatenate([spring_lo, leak_lo], axis=0), along_j
-    )
-    on_b = dot(sums_a, jnp.concatenate([spring_hi, leak_hi], axis=1), along_i) + dot(
-        sums_a, jnp.concatenate([spring_lo, leak_lo], axis=1), along_i
-    )
-    return on_a, on_b
+    return spring_hi, leak_hi, spring_lo, leak_lo
 
 
 def kernel(
     nreg,
     nbulk,
+    pos_hbm,
+    fld_hbm,
+    sto_hbm,
+    vel_hbm,
+    send_hbm,
+    touch_hbm,
+    pair_hbm,
+    move_hbm,
+    rmask_hbm,
+    lmask_hbm,
+    nf_ref,
+    nv_ref,
+    arr_ref,
     pos_ref,
     fld_ref,
     sto_ref,
@@ -140,9 +150,6 @@
     pair_v,
     rmask_ref,
     lmask_ref,
-    nf_ref,
-    nv_ref,
-    arr_ref,
     pts,
     stage,
     got,
@@ -153,7 +160,12 @@
     left,
     right,
     sums,
+    rleft,
+    rsums,
     terms,
+    dists,
+    weights,
+    load_sem,
     send1,
     recv1,
     send2,
@@ -181,15 +193,39 @@
                 continue
             peers.append((o, lax.rem(me + step, nbulk)))
 
+    loads = {}
+    for n, (name, src, dst) in enumerate(
+        (
+            ("send_s", send_hbm, send_s),
+            ("pos", pos_hbm, pos_ref),
+            ("fld", fld_hbm, fld_ref),
+            ("pair_s", pair_hbm, pair_s),
+            ("lmask", lmask_hbm, lmask_ref),
+            ("touch_s", touch_hbm, touch_s),
+            ("rmask", rmask_hbm, rmask_ref),
+            ("vel", vel_hbm, vel_ref),
+            ("sto", sto_hbm, sto_ref),
+            ("move_s", move_hbm, move_s),
+            ("send_v", send_hbm, send_v),
+            ("touch_v", touch_hbm, touch_v),
+            ("pair_v", pair_hbm, pair_v),
+        )
+    ):
+        loads[name] = pltpu.make_async_copy(src, dst, load_sem.at[n])
+        loads[name].start()
+
     barrier = pltpu.get_barrier_semaphore()
     for o, d in peers:
         pl.semaphore_signal(barrier, inc=1, device_id=(region_at(o - 1), d), device_id_type=MESH)
 
+    loads["pos"].wait()
+    loads["fld"].wait()
     for k in range(3):
         pts[:, k, :] = pos_ref[k]
     for k in range(4):
         pts[:, 3 + k, :] = fld_ref[:, k, :]
     pts[:, 7, :] = jnp.zeros((blocks, width), F32)
+    loads["send_s"].wait()
     for o in range(3):
         for s in range(slots):
             for d in range(nbulk):
@@ -253,81 +289,132 @@
     def put(t, value):
         terms[:, pl.ds(t, 1), :] = value[0:4].reshape(4, 1, width)
 
-    def local(t):
-        a = pair_s[0, t]
-        b = pair_s[1, t]
-        on_a, on_b = tile(left[b], right[a], sums[b], sums[a], lmask_ref[t])
-        put(t, combine(pts[a], on_a))
-        put(pairs + t, combine(pts[b], on_b))
-
-    def locals_(step, carry):
-        local(2 * step)
-        local(2 * step + 1)
-        return carry
-
-    lax.fori_loop(0, pairs // 2, locals_, 0)
-
-    def remote(q, carry):
-        o = q // per
-        b = lax.rem(q, per) // slots
-        s = lax.rem(q, slots)
-        own = (o == 1) & (b == me)
-
-        if slots == 1:
-            @pl.when(jnp.logical_not(own))
-            def _():
-                arrival(got, recv1, o, b)
-        else:
-            @pl.when(jnp.logical_not(own) & (s == 0))
-            def _():
-                arrival(got, recv1, o, b)
-
-        block = got[o, lax.rem(q, per)]
-        left_b, _, sums_b = features(block[None])
-        total = None
-        for t in range(touch):
-            a = touch_s[t, q]
-            on_a, on_b = tile(left_b[0], right[a], sums_b[0], sums[a], rmask_ref[q, t])
-            put(base + t * recv_count + q, combine(pts[a], on_a))
-            total = on_b if total is None else total + on_b
-        back[o, lax.rem(q, per)] = combine(block, total)
-
-        @pl.when(jnp.logical_not(own) & (s == slots - 1))
-        def _():
-            copy2(o, b).start()
-
-        return carry
-
-    lax.fori_loop(0, recv_count, remote, 0)
+    def stages(first, count, measure, weigh, add):
+        def body(i, carry):
+            add(jnp.maximum(i - 2, first))
+            weigh(jnp.clip(i - 1, first, first + count - 1))
+            measure(jnp.minimum(i, first + count - 1))
+            return carry
+
+        lax.fori_loop(first, first + count + 2, body, 0)
+
+    def weigh_into(u, packed):
+        s_hi, l_hi, s_lo, l_lo = split_weights(dists[u], packed)
+        weights[u, 0, 0:width] = s_hi
+        weights[u, 0, width:] = l_hi
+        weights[u, 1, 0:width] = s_lo
+        weights[u, 1, width:] = l_lo
+
+    def add_tile(u, sums_a, sums_b):
+        on_a = dot(sums_b, weights[u, 0], ALONG_J) + dot(sums_b, weights[u, 1], ALONG_J)
+        on_b = None
+        for piece in range(2):
+            both = jnp.concatenate([weights[u, piece, 0:width], weights[u, piece, width:]], axis=1)
+            part = dot(sums_a, both, ALONG_I)
+            on_b = part if on_b is None else on_b + part
+        return on_a, on_b
+
+    lane = 4
+
+    def local_measure(i):
+        for u in range(lane):
+            t = lane * i + u
+            dists[u] = distance(left[pair_s[1, t]], right[pair_s[0, t]])
+
+    def local_weigh(i):
+        for u in range(lane):
+            weigh_into(u, lmask_ref[lane * i + u])
+
+    def local_add(i):
+        for u in range(lane):
+            t = lane * i + u
+            a = pair_s[0, t]
+            b = pair_s[1, t]
+            on_a, on_b = add_tile(u, sums[a], sums[b])
+            put(t, combine(pts[a], on_a))
+            put(pairs + t, combine(pts[b], on_b))
+
+    loads["pair_s"].wait()
+    loads["lmask"].wait()
+    local_count = pairs // lane
+    early = local_count // 2
+    stages(0, early, local_measure, local_weigh, local_add)
+
+    loads["touch_s"].wait()
+    loads["rmask"].wait()
+    for o, d in peers:
+        arrival(got, recv1, o, d)
+    for o in range(3):
+        for step in range(per // group):
+            at = pl.ds(step * group, group)
+            to = pl.ds(o * per + step * group, group)
+            rleft[to], _, rsums[to] = features(got[o, at])
+    near = lane // touch
+
+    def remote_measure(i):
+        for v in range(near):
+            q = near * i + v
+            for t in range(touch):
+                dists[touch * v + t] = distance(rleft[q], right[touch_s[t, q]])
+
+    def remote_weigh(i):
+        for v in range(near):
+            for t in range(touch):
+                weigh_into(touch * v + t, rmask_ref[near * i + v, t])
+
+    def remote_add(i):
+        for v in range(near):
+            q = near * i + v
+            total = None
+            for t in range(touch):
+                a = touch_s[t, q]
+                on_a, on_b = add_tile(touch * v + t, sums[a], rsums[q])
+                put(base + t * recv_count + q, combine(pts[a], on_a))
+                total = on_b if total is None else total + on_b
+            o = q // per
+            at = lax.rem(q, per)
+            back[o, at] = combine(got[o, at], total)
+
+    stages(0, recv_count // near, remote_measure, remote_weigh, remote_add)
+    for o, d in peers:
+        copy2(o, d).start()
     for s in range(slots):
         ret[1, me * slots + s] = back[1, me * slots + s]
-    for o, d in peers:
-        arrival(ret, recv2, o, d)
-    for o in range(3):
-        for d in range(per):
-            put(base + touch * recv_count + o * per + d, ret[o, d])
-
+    stages(early, local_count - early, local_measure, local_weigh, local_add)
+
+    loads["send_v"].wait()
+    loads["touch_v"].wait()
+    loads["pair_v"].wait()
     index = jnp.concatenate(
         [pair_v[0:1], pair_v[1:2]]
         + [touch_v[t : t + 1] for t in range(touch)]
-        + [send_v[o] for o in range(3)]
+        + [send_v[o, s : s + 1] for o in range(3) for s in range(slots)]
         + [jnp.full((1, rows - used), -1, jnp.int32)],
         axis=1,
     )
     here = lax.broadcasted_iota(jnp.int32, (blocks, rows), 0)
     pick = jnp.where(here == index, 1.0, 0.0).astype(BF16)
+    for o, d in peers:
+        arrival(ret, recv2, o, d)
+    for o in range(3):
+        for s in range(slots):
+            for d in range(nbulk):
+                put(base + touch * recv_count + (o * slots + s) * nbulk + d, ret[o, d * slots + s])
     totals = []
     for k in range(4):
         parts = split3(terms[k])
         totals.append(
             sum(jnp.dot(pick, part.astype(BF16), preferred_element_type=F32) for part in parts)
         )
+    loads["vel"].wait()
+    loads["sto"].wait()
     for k in range(3):
         speed = vel_ref[k] + time_step * totals[k]
         nv_ref[k] = speed
         nf_ref[:, k, :] = fld_ref[:, k, :] + time_step * speed
     nf_ref[:, 3, :] = fld_ref[:, 3, :] + time_step * totals[3] / sto_ref[...]
 
+    loads["move_s"].wait()
     for d in range(nbulk):
         for m in range(mig):
             entry = move_s[m, 0, d]
@@ -384,7 +471,6 @@
         pair_rows = local_pairs[0].T
         moves = migrate_list[0].T[:, None, :]
         vmem = pl.BlockSpec(memory_space=pltpu.VMEM)
-        smem = pl.BlockSpec(memory_space=pltpu.SMEM)
         dma = pltpu.SemaphoreType.DMA
         new_fields, speed, arrived = pl.pallas_call(
             functools.partial(kernel, nreg, nbulk),
@@ -393,9 +479,22 @@
                 jax.ShapeDtypeStruct((3, blocks, width), F32),
                 jax.ShapeDtypeStruct((11, nbulk * mig, width), F32),
             ),
-            in_specs=[vmem] * 4 + [smem] * 4 + [vmem] * 5,
+            in_specs=[pl.BlockSpec(memory_space=pltpu.HBM)] * 10,
             out_specs=(vmem, vmem, vmem),
             scratch_shapes=[
+                pltpu.VMEM((3, blocks, width), F32),
+                pltpu.VMEM((blocks, 4, width), F32),
+                pltpu.VMEM((blocks, width), F32),
+                pltpu.VMEM((3, blocks, width), F32),
+                pltpu.SMEM(sends.shape, jnp.int32),
+                pltpu.SMEM(touches.shape, jnp.int32),
+                pltpu.SMEM(pair_rows.shape, jnp.int32),
+                pltpu.SMEM(moves.shape, jnp.int32),
+                pltpu.VMEM(sends.shape, jnp.int32),
+                pltpu.VMEM(touches.shape, jnp.int32),
+                pltpu.VMEM(pair_rows.shape, jnp.int32),
+                pltpu.VMEM(remote_mask.shape[1:], jnp.int32),
+                pltpu.VMEM(local_mask.shape[1:], jnp.int32),
                 pltpu.VMEM((blocks, 8, width), F32),
                 pltpu.VMEM((3, per, 8, width), F32),
                 pltpu.VMEM((3, per, 8, width), F32),
@@ -406,7 +505,12 @@
                 pltpu.VMEM((blocks, 48, width), BF16),
                 pltpu.VMEM((blocks, 48, width), BF16),
                 pltpu.VMEM((blocks, 16, 2 * width), BF16),
+                pltpu.VMEM((recv_count, 48, width), BF16),
+                pltpu.VMEM((recv_count, 16, 2 * width), BF16),
                 pltpu.VMEM((4, rows, width), F32),
+                pltpu.VMEM((4, width, width), F32),
+                pltpu.VMEM((4, 2, 2 * width, width), BF16),
+                dma((13,)),
                 dma((3, nbulk)),
                 dma((3, nbulk)),
                 dma((3, nbulk)),
@@ -415,7 +519,7 @@
                 dma((nbulk,)),
             ],
             compiler_params=pltpu.CompilerParams(
-                collective_id=0, has_side_effects=True, vmem_limit_bytes=32 << 20
+                collective_id=0, has_side_effects=True, vmem_limit_bytes=64 << 20
             ),
         )(
             positions.transpose(1, 0, 2),
@@ -426,9 +530,6 @@
             touches,
             pair_rows,
             moves,
-            sends,
-            touches,
-            pair_rows,
             remote_mask[0],
             local_mask[0],
         )

time: 56.5 us -> 31 us (0.55)
  Pallas kernels: 47.3 us -> 27.2 us
  local copies, waits for them, and re-layouts: 8.09 us -> 3.01 us
    pallas_call x1, Pallas kernels: 47.3 us -> 27.2 us  [per_device(): pl.pallas_call(functools.partial(kernel, nreg, nbulk), out_shape=(jax.Sha...]
    unnamed x23 -> x7, local copies, waits for them, and re-layouts: 8.09 us -> 3.01 us
where the time goes in v2:
time: 31 us; the launch traced here: 30.8 us
  Pallas kernels  27.2 us (88%)
  local copies, waits for them, and re-layouts  3.01 us (10%)
  between operations  0.65 us (2%)
    pallas_call x1, Pallas kernels, per_device(): pl.pallas_call(functools.partial(kernel, nreg, nbulk), out_shape=(jax.Sha...  27.2 us
    unnamed x7, local copies, waits for them, and re-layouts  3.01 us

profile of v2, /device:TPU:0, one launch (start us, length us, event | category | flops | bytes accessed | tf_op | source)
XLA Modules:
  0.0 30.8 jit_solution(7401734613168914131)
XLA Ops:
  0.6 27.2 %shard_map.121 = (f32[64,4,128]{2,1,0:T(4,128)}, f32[3,64,128]{2,1,0:T(8,128)}, f32[11,8,128]{2,1,0:T(8,128)}) custom-call(f32[3,64,128]{2,1,0:T(8,128)} %bitcast.16, f32[64,4,128]{2,1,0:T(4,128)} %fld_hbm.1, f32[64,128]{1,0:T(8,128)} %sto_hbm.1, f32[3,64,128]{2,1,0:T(8,128)} %bitcast.17, s32[3,1,8]{2,1,0:T(1,128)} %bitcast.20, s32[2,24]{1,0:T(2,128)} %bitcast.21, ...), custom_call_target="tpu_custom_call" | custom-call | tf_op jit(solution)/shard_map/pallas_call | solution.py:475
  27.8 0.0 copy-start
  27.8 1.6 %copy.16 = f32[64,4,128]{2,1,0:T(4,128)} copy(f32[64,4,128]{2,1,0:T(4,128)} %get-tuple-element.12) | data formatting | bytes 262144
  29.4 0.0 copy-done
  29.4 0.0 copy-start.1
  29.4 0.6 %copy.17 = f32[64,3,128]{2,0,1:T(8,128)} copy(f32[64,3,128]{2,0,1:T(8,128)S(1)} %bitcast.18) | data formatting | bytes 196608
  30.1 0.1 copy-done.1
  30.2 0.6 %copy.18 = f32[8,11,128]{2,0,1:T(8,128)} copy(f32[8,11,128]{2,0,1:T(8,128)S(1)} %bitcast.19) | data formatting | bytes 90112
Async XLA Ops:
  27.8 1.6 %copy-start = (f32[3,64,128]{2,1,0:T(8,128)S(1)}, f32[3,64,128]{2,1,0:T(8,128)}, u32[]{:S(2)}) copy-start(f32[3,64,128]{2,1,0:T(8,128)} %get-tuple-element.7) | copy-start | bytes 294916
  29.4 0.8 %copy-start.1 = (f32[11,8,128]{2,1,0:T(8,128)S(1)}, f32[11,8,128]{2,1,0:T(8,128)}, u32[]{:S(2)}) copy-start(f32[11,8,128]{2,1,0:T(8,128)} %get-tuple-element.8) | copy-start | bytes 135172

commit v3 on v2

--- a/solution.py
+++ b/solution.py
@@ -12,6 +12,7 @@
 leak_gain = 0.5
 time_step = 0.5
 half_press = 0.025
+LANES = 4
 F32 = jnp.float32
 BF16 = jnp.bfloat16
 
@@ -148,8 +149,7 @@
     send_v,
     touch_v,
     pair_v,
-    rmask_ref,
-    lmask_ref,
+    masks,
     pts,
     stage,
     got,
@@ -160,9 +160,9 @@
     left,
     right,
     sums,
-    rleft,
-    rsums,
-    terms,
+    tab,
+    aterm,
+    bterm,
     dists,
     weights,
     load_sem,
@@ -200,9 +200,9 @@
             ("pos", pos_hbm, pos_ref),
             ("fld", fld_hbm, fld_ref),
             ("pair_s", pair_hbm, pair_s),
-            ("lmask", lmask_hbm, lmask_ref),
+            ("lmask", lmask_hbm, masks.at[pl.ds(0, pairs)]),
             ("touch_s", touch_hbm, touch_s),
-            ("rmask", rmask_hbm, rmask_ref),
+            ("rmask", rmask_hbm, masks.at[pl.ds(pairs, touch * recv_count)]),
             ("vel", vel_hbm, vel_ref),
             ("sto", sto_hbm, sto_ref),
             ("move_s", move_hbm, move_s),
@@ -221,10 +221,10 @@
     loads["pos"].wait()
     loads["fld"].wait()
     for k in range(3):
-        pts[:, k, :] = pos_ref[k]
+        pts[0:blocks, k, :] = pos_ref[k]
     for k in range(4):
-        pts[:, 3 + k, :] = fld_ref[:, k, :]
-    pts[:, 7, :] = jnp.zeros((blocks, width), F32)
+        pts[0:blocks, 3 + k, :] = fld_ref[:, k, :]
+    pts[0:blocks, 7, :] = jnp.zeros((blocks, width), F32)
     loads["send_s"].wait()
     for o in range(3):
         for s in range(slots):
@@ -281,110 +281,118 @@
         return carry
 
     lax.fori_loop(0, blocks // group, build, 0)
-    base = 2 * pairs
-    used = base + touch * recv_count + recv_count
-    rows = terms.shape[1]
-    terms[:, base:, :] = jnp.zeros((4, rows - base, width), F32)
-
-    def put(t, value):
-        terms[:, pl.ds(t, 1), :] = value[0:4].reshape(4, 1, width)
-
-    def stages(first, count, measure, weigh, add):
-        def body(i, carry):
-            add(jnp.maximum(i - 2, first))
-            weigh(jnp.clip(i - 1, first, first + count - 1))
-            measure(jnp.minimum(i, first + count - 1))
-            return carry
-
-        lax.fori_loop(first, first + count + 2, body, 0)
-
-    def weigh_into(u, packed):
-        s_hi, l_hi, s_lo, l_lo = split_weights(dists[u], packed)
-        weights[u, 0, 0:width] = s_hi
-        weights[u, 0, width:] = l_hi
-        weights[u, 1, 0:width] = s_lo
-        weights[u, 1, width:] = l_lo
-
-    def add_tile(u, sums_a, sums_b):
-        on_a = dot(sums_b, weights[u, 0], ALONG_J) + dot(sums_b, weights[u, 1], ALONG_J)
-        on_b = None
-        for piece in range(2):
-            both = jnp.concatenate([weights[u, piece, 0:width], weights[u, piece, width:]], axis=1)
-            part = dot(sums_a, both, ALONG_I)
-            on_b = part if on_b is None else on_b + part
-        return on_a, on_b
-
-    lane = 4
-
-    def local_measure(i):
-        for u in range(lane):
-            t = lane * i + u
-            dists[u] = distance(left[pair_s[1, t]], right[pair_s[0, t]])
-
-    def local_weigh(i):
-        for u in range(lane):
-            weigh_into(u, lmask_ref[lane * i + u])
-
-    def local_add(i):
-        for u in range(lane):
-            t = lane * i + u
-            a = pair_s[0, t]
-            b = pair_s[1, t]
-            on_a, on_b = add_tile(u, sums[a], sums[b])
-            put(t, combine(pts[a], on_a))
-            put(pairs + t, combine(pts[b], on_b))
 
     loads["pair_s"].wait()
+    loads["touch_s"].wait()
+    for t in range(pairs):
+        tab[0, t] = pair_s[0, t]
+        tab[1, t] = pair_s[1, t]
+    for q in range(recv_count):
+        for t in range(touch):
+            tab[0, pairs + touch * q + t] = touch_s[t, q]
+            tab[1, pairs + touch * q + t] = blocks + q
     loads["lmask"].wait()
-    local_count = pairs // lane
-    early = local_count // 2
-    stages(0, early, local_measure, local_weigh, local_add)
-
-    loads["touch_s"].wait()
     loads["rmask"].wait()
-    for o, d in peers:
-        arrival(got, recv1, o, d)
-    for o in range(3):
-        for step in range(per // group):
-            at = pl.ds(step * group, group)
-            to = pl.ds(o * per + step * group, group)
-            rleft[to], _, rsums[to] = features(got[o, at])
-    near = lane // touch
-
-    def remote_measure(i):
-        for v in range(near):
-            q = near * i + v
-            for t in range(touch):
-                dists[touch * v + t] = distance(rleft[q], right[touch_s[t, q]])
-
-    def remote_weigh(i):
-        for v in range(near):
-            for t in range(touch):
-                weigh_into(touch * v + t, rmask_ref[near * i + v, t])
-
-    def remote_add(i):
-        for v in range(near):
-            q = near * i + v
-            total = None
-            for t in range(touch):
-                a = touch_s[t, q]
-                on_a, on_b = add_tile(touch * v + t, sums[a], rsums[q])
-                put(base + t * recv_count + q, combine(pts[a], on_a))
-                total = on_b if total is None else total + on_b
-            o = q // per
-            at = lax.rem(q, per)
-            back[o, at] = combine(got[o, at], total)
-
-    stages(0, recv_count // near, remote_measure, remote_weigh, remote_add)
-    for o, d in peers:
-        copy2(o, d).start()
+
+    local_groups = pairs // LANES
+    remote_groups = touch * recv_count // LANES
+    count = local_groups + remote_groups
+    early = local_groups // 2
+    begin = early
+    done = early + remote_groups
+
+    def first_tile(i):
+        shifted = jnp.where(
+            i < begin, i, jnp.where(i < done, i + (local_groups - early), i - remote_groups)
+        )
+        return LANES * shifted
+
+    def measure(first):
+        for u in range(0, LANES, 2):
+            f, g = [], []
+            for v in (u, u + 1):
+                f.append(left[tab[1, first + v]])
+                g.append(right[tab[0, first + v]])
+            blank = jnp.zeros_like(g[0])
+            lhs = jnp.concatenate(f, axis=0)
+            rhs = jnp.concatenate(
+                [
+                    jnp.concatenate([g[0], blank], axis=1),
+                    jnp.concatenate([blank, g[1]], axis=1),
+                ],
+                axis=0,
+            )
+            dists[u // 2] = distance(lhs, rhs)
+
+    def weigh(first):
+        for u in range(LANES):
+            cols = slice((u % 2) * width, (u % 2 + 1) * width)
+            s_hi, l_hi, s_lo, l_lo = split_weights(dists[u // 2, :, cols], masks[first + u])
+            weights[u // 2, 0, 0:width, cols] = s_hi
+            weights[u // 2, 0, width:, cols] = l_hi
+            weights[u // 2, 1, 0:width, cols] = s_lo
+            weights[u // 2, 1, width:, cols] = l_lo
+
+    def add(first):
+        for u in range(0, LANES, 2):
+            ids = [[tab[side, first + v] for v in (u, u + 1)] for side in range(2)]
+            v_a = jnp.concatenate([sums[at] for at in ids[0]], axis=0)
+            v_b = jnp.concatenate([sums[at] for at in ids[1]], axis=0)
+            on_a = on_b = None
+            for piece in range(2):
+                w = weights[u // 2, piece]
+                turned = jnp.concatenate(
+                    [
+                        jnp.concatenate([w[:width, :width], w[width:, :width]], axis=1),
+                        jnp.concatenate([w[:width, width:], w[width:, width:]], axis=1),
+                    ],
+                    axis=0,
+                )
+                part_a = dot(v_b, w, ALONG_J)
+                part_b = dot(v_a, turned, ALONG_I)
+                on_a = part_a if on_a is None else on_a + part_a
+                on_b = part_b if on_b is None else on_b + part_b
+            for v in range(2):
+                rows16 = slice(16 * v, 16 * v + 16)
+                cols = slice(v * width, (v + 1) * width)
+                aterm[first + u + v] = combine(pts[ids[0][v]], on_a[rows16, cols])
+                bterm[first + u + v] = combine(pts[ids[1][v]], on_b[rows16, cols])
+
+    def body(i, carry):
+        @pl.when(i == begin)
+        def _():
+            for o, d in peers:
+                arrival(got, recv1, o, d)
+            for o in range(3):
+                for step in range(per // group):
+                    block = got[o, step * group : (step + 1) * group]
+                    to = pl.ds(blocks + o * per + step * group, group)
+                    pts[to] = block
+                    left[to], _, sums[to] = features(block)
+
+        @pl.when(i == done + 2)
+        def _():
+            for o in range(3):
+                for s in range(per):
+                    at = pairs + touch * (o * per + s)
+                    back[o, s] = sum(bterm[at + t] for t in range(touch))
+            for o, d in peers:
+                copy2(o, d).start()
+
+        add(first_tile(jnp.maximum(i - 2, 0)))
+        weigh(first_tile(jnp.clip(i - 1, 0, count - 1)))
+        measure(first_tile(jnp.minimum(i, count - 1)))
+        return carry
+
+    lax.fori_loop(0, count + 2, body, 0)
     for s in range(slots):
         ret[1, me * slots + s] = back[1, me * slots + s]
-    stages(early, local_count - early, local_measure, local_weigh, local_add)
 
     loads["send_v"].wait()
     loads["touch_v"].wait()
     loads["pair_v"].wait()
+    used = 2 * pairs + (touch + 1) * recv_count
+    rows = -(-used // 128) * 128
     index = jnp.concatenate(
         [pair_v[0:1], pair_v[1:2]]
         + [touch_v[t : t + 1] for t in range(touch)]
@@ -396,13 +404,21 @@
     pick = jnp.where(here == index, 1.0, 0.0).astype(BF16)
     for o, d in peers:
         arrival(ret, recv2, o, d)
-    for o in range(3):
-        for s in range(slots):
-            for d in range(nbulk):
-                put(base + touch * recv_count + (o * slots + s) * nbulk + d, ret[o, d * slots + s])
+
+    def plane(k):
+        found = [aterm[0:pairs, k, :], bterm[0:pairs, k, :]]
+        found += [aterm[pl.ds(pairs + t, recv_count, touch), k, :] for t in range(touch)]
+        if slots == 1:
+            found += [ret[o, :, k, :] for o in range(3)]
+        else:
+            found += [
+                ret[o, pl.ds(s, nbulk, slots), k, :] for o in range(3) for s in range(slots)
+            ]
+        return jnp.concatenate(found + [jnp.zeros((rows - used, width), F32)], axis=0)
+
     totals = []
     for k in range(4):
-        parts = split3(terms[k])
+        parts = split3(plane(k))
         totals.append(
             sum(jnp.dot(pick, part.astype(BF16), preferred_element_type=F32) for part in parts)
         )
@@ -465,7 +481,8 @@
         pairs = local_pairs.shape[1]
         mig = migrate_list.shape[2]
         per = nbulk * slots
-        rows = -(-(2 * pairs + (touch + 1) * recv_count) // 128) * 128
+        tiles = pairs + touch * recv_count
+        held = blocks + recv_count
         sends = send_list[0].transpose(0, 2, 1)
         touches = remote_local[0].T
         pair_rows = local_pairs[0].T
@@ -493,23 +510,22 @@
                 pltpu.VMEM(sends.shape, jnp.int32),
                 pltpu.VMEM(touches.shape, jnp.int32),
                 pltpu.VMEM(pair_rows.shape, jnp.int32),
-                pltpu.VMEM(remote_mask.shape[1:], jnp.int32),
-                pltpu.VMEM(local_mask.shape[1:], jnp.int32),
-                pltpu.VMEM((blocks, 8, width), F32),
+                pltpu.VMEM((tiles,) + local_mask.shape[2:], jnp.int32),
+                pltpu.VMEM((held, 8, width), F32),
                 pltpu.VMEM((3, per, 8, width), F32),
                 pltpu.VMEM((3, per, 8, width), F32),
                 pltpu.VMEM((3, per, 8, width), F32),
                 pltpu.VMEM((3, per, 8, width), F32),
                 pltpu.VMEM((nbulk * mig, 16, width), F32),
                 pltpu.VMEM((nbulk * mig, 16, width), F32),
+                pltpu.VMEM((held, 48, width), BF16),
                 pltpu.VMEM((blocks, 48, width), BF16),
-                pltpu.VMEM((blocks, 48, width), BF16),
-                pltpu.VMEM((blocks, 16, 2 * width), BF16),
-                pltpu.VMEM((recv_count, 48, width), BF16),
-                pltpu.VMEM((recv_count, 16, 2 * width), BF16),
-                pltpu.VMEM((4, rows, width), F32),
-                pltpu.VMEM((4, width, width), F32),
-                pltpu.VMEM((4, 2, 2 * width, width), BF16),
+                pltpu.VMEM((held, 16, 2 * width), BF16),
+                pltpu.SMEM((2, tiles), jnp.int32),
+                pltpu.VMEM((tiles, 8, width), F32),
+                pltpu.VMEM((tiles, 8, width), F32),
+                pltpu.VMEM((LANES // 2, width, 2 * width), F32),
+                pltpu.VMEM((LANES // 2, 2, 2 * width, 2 * width), BF16),
                 dma((13,)),
                 dma((3, nbulk)),
                 dma((3, nbulk)),
@@ -530,7 +546,7 @@
             touches,
             pair_rows,
             moves,
-            remote_mask[0],
+            remote_mask[0].reshape((touch * recv_count,) + remote_mask.shape[3:]),
             local_mask[0],
         )
         return new_fields, speed.transpose(1, 0, 2), arrived.transpose(1, 0, 2)

time: 31 us -> 32.2 us (1.039)
  Pallas kernels: 27.2 us -> 28.3 us
    pallas_call x1, Pallas kernels: 27.2 us -> 28.3 us  [per_device(): pl.pallas_call(functools.partial(kernel, nreg, nbulk), out_shape=(jax.Sha...]
where the time goes in v3:
time: 32.2 us; the launch traced here: 32 us
  Pallas kernels  28.3 us (88%)
  local copies, waits for them, and re-layouts  3.01 us (9%)
  between operations  0.65 us (2%)
    pallas_call x1, Pallas kernels, per_device(): pl.pallas_call(functools.partial(kernel, nreg, nbulk), out_shape=(jax.Sha...  28.3 us
    unnamed x7, local copies, waits for them, and re-layouts  3.01 us

profile of v3, /device:TPU:0, one launch (start us, length us, event | category | flops | bytes accessed | tf_op | source)
XLA Modules:
  0.0 32.0 jit_solution(41647089588615886)
XLA Ops:
  0.6 28.3 %shard_map.121 = (f32[64,4,128]{2,1,0:T(4,128)}, f32[3,64,128]{2,1,0:T(8,128)}, f32[11,8,128]{2,1,0:T(8,128)}) custom-call(f32[3,64,128]{2,1,0:T(8,128)} %bitcast.16, f32[64,4,128]{2,1,0:T(4,128)} %fld_hbm.1, f32[64,128]{1,0:T(8,128)} %sto_hbm.1, f32[3,64,128]{2,1,0:T(8,128)} %bitcast.17, s32[3,1,8]{2,1,0:T(1,128)} %bitcast.20, s32[2,24]{1,0:T(2,128)} %bitcast.21, ...), custom_call_target="tpu_custom_call" | custom-call | tf_op jit(solution)/shard_map/pallas_call | solution.py:492
  28.9 0.0 copy-start
  29.0 1.6 %copy.16 = f32[64,4,128]{2,1,0:T(4,128)} copy(f32[64,4,128]{2,1,0:T(4,128)} %get-tuple-element.12) | data formatting | bytes 262144
  30.6 0.0 copy-done
  30.6 0.0 copy-start.1
  30.6 0.6 %copy.17 = f32[64,3,128]{2,0,1:T(8,128)} copy(f32[64,3,128]{2,0,1:T(8,128)S(1)} %bitcast.18) | data formatting | bytes 196608
  31.2 0.1 copy-done.1
  31.4 0.6 %copy.18 = f32[8,11,128]{2,0,1:T(8,128)} copy(f32[8,11,128]{2,0,1:T(8,128)S(1)} %bitcast.19) | data formatting | bytes 90112
Async XLA Ops:
  28.9 1.6 %copy-start = (f32[3,64,128]{2,1,0:T(8,128)S(1)}, f32[3,64,128]{2,1,0:T(8,128)}, u32[]{:S(2)}) copy-start(f32[3,64,128]{2,1,0:T(8,128)} %get-tuple-element.7) | copy-start | bytes 294916
  30.6 0.8 %copy-start.1 = (f32[11,8,128]{2,1,0:T(8,128)S(1)}, f32[11,8,128]{2,1,0:T(8,128)}, u32[]{:S(2)}) copy-start(f32[11,8,128]{2,1,0:T(8,128)} %get-tuple-element.8) | copy-start | bytes 135172

commit v4 on v3

--- a/solution.py
+++ b/solution.py
@@ -12,7 +12,7 @@
 leak_gain = 0.5
 time_step = 0.5
 half_press = 0.025
-LANES = 4
+LANES = 8
 F32 = jnp.float32
 BF16 = jnp.bfloat16
 

time: 32.2 us -> 32.2 us (level)
  no operation moved by 1% of the time
where the time goes in v4:
time: 32.2 us; the launch traced here: 32 us
  Pallas kernels  28.3 us (88%)
  local copies, waits for them, and re-layouts  3.01 us (9%)
  between operations  0.65 us (2%)
    pallas_call x1, Pallas kernels, per_device(): pl.pallas_call(functools.partial(kernel, nreg, nbulk), out_shape=(jax.Sha...  28.3 us
    unnamed x7, local copies, waits for them, and re-layouts  3.01 us

profile of v4, /device:TPU:0, one launch (start us, length us, event | category | flops | bytes accessed | tf_op | source)
XLA Modules:
  0.0 32.0 jit_solution(6218612274915089969)
XLA Ops:
  0.6 28.3 %shard_map.121 = (f32[64,4,128]{2,1,0:T(4,128)}, f32[3,64,128]{2,1,0:T(8,128)}, f32[11,8,128]{2,1,0:T(8,128)}) custom-call(f32[3,64,128]{2,1,0:T(8,128)} %bitcast.16, f32[64,4,128]{2,1,0:T(4,128)} %fld_hbm.1, f32[64,128]{1,0:T(8,128)} %sto_hbm.1, f32[3,64,128]{2,1,0:T(8,128)} %bitcast.17, s32[3,1,8]{2,1,0:T(1,128)} %bitcast.20, s32[2,24]{1,0:T(2,128)} %bitcast.21, ...), custom_call_target="tpu_custom_call" | custom-call | tf_op jit(solution)/shard_map/pallas_call | solution.py:492
  28.9 0.0 copy-start
  28.9 1.6 %copy.16 = f32[64,4,128]{2,1,0:T(4,128)} copy(f32[64,4,128]{2,1,0:T(4,128)} %get-tuple-element.12) | data formatting | bytes 262144
  30.5 0.0 copy-done
  30.5 0.0 copy-start.1
  30.5 0.6 %copy.17 = f32[64,3,128]{2,0,1:T(8,128)} copy(f32[64,3,128]{2,0,1:T(8,128)S(1)} %bitcast.18) | data formatting | bytes 196608
  31.2 0.1 copy-done.1
  31.3 0.6 %copy.18 = f32[8,11,128]{2,0,1:T(8,128)} copy(f32[8,11,128]{2,0,1:T(8,128)S(1)} %bitcast.19) | data formatting | bytes 90112
Async XLA Ops:
  28.9 1.6 %copy-start = (f32[3,64,128]{2,1,0:T(8,128)S(1)}, f32[3,64,128]{2,1,0:T(8,128)}, u32[]{:S(2)}) copy-start(f32[3,64,128]{2,1,0:T(8,128)} %get-tuple-element.7) | copy-start | bytes 294916
  30.5 0.8 %copy-start.1 = (f32[11,8,128]{2,1,0:T(8,128)S(1)}, f32[11,8,128]{2,1,0:T(8,128)}, u32[]{:S(2)}) copy-start(f32[11,8,128]{2,1,0:T(8,128)} %get-tuple-element.8) | copy-start | bytes 135172

commit v5 on v4

--- a/solution.py
+++ b/solution.py
@@ -13,6 +13,7 @@
 time_step = 0.5
 half_press = 0.025
 LANES = 8
+PACK = 4
 F32 = jnp.float32
 BF16 = jnp.bfloat16
 
@@ -40,12 +41,25 @@
     row = rows_of(block.shape)
     half = jnp.where(row < 3, 0.5 * block, 0.0)
     norm = jnp.sum(half * half, axis=-2, keepdims=True) + 0.5
-    as_b = jnp.where(row == 3, norm, jnp.where(row == 4, 1.0, half))
-    as_a = jnp.where(row == 3, 1.0, jnp.where(row == 4, norm, -2.0 * half))
-    b1, b2, b3 = split3(as_b)
-    a1, a2, a3 = split3(as_a)
-    left = jnp.concatenate([b1, b1, b2, b2, b1, b3], axis=-2).astype(BF16)
-    right = jnp.concatenate([a1, a2, a1, a2, a3, a1], axis=-2).astype(BF16)
+    h1, h2, h3 = split3(half)
+    n1, n2, n3 = split3(norm)
+
+    def eight(first, second, second_last, last):
+        return jnp.where(
+            row < 6, first + roll(second, 3), jnp.where(row == 6, second_last, last)
+        )
+
+    blank = jnp.zeros_like(half)
+    b_rows = [eight(h1, h1, n1, 1.0), eight(h2, h2, n2, 1.0), eight(h1, h3, n3, 1.0), blank]
+    a_rows = [
+        eight(-2.0 * h1, -2.0 * h2, 1.0, n1),
+        eight(-2.0 * h1, -2.0 * h2, 1.0, n2),
+        eight(-2.0 * h3, -2.0 * h1, 1.0, n3),
+        blank,
+    ]
+    flat = jnp.concatenate(b_rows, axis=-2).reshape(-1, PACK * 32, block.shape[-1])
+    left = jnp.stack([flat[n].T for n in range(flat.shape[0])]).astype(BF16)
+    right = jnp.concatenate(a_rows, axis=-2).astype(BF16)
     press = block[..., 6:7, :]
     moved = roll(block, -3)
     product = -0.25 * press * block
@@ -102,8 +116,9 @@
 dot = functools.partial(lax.dot_general, preferred_element_type=F32)
 
 
-def distance(left_b, right_a):
-    return dot(left_b, right_a, (((0,), (0,)), ((), ())))
+def distance(left_b, right_a, part):
+    spread = [jnp.where(part == k, right_a, jnp.zeros_like(right_a)) for k in range(PACK)]
+    return dot(left_b, jnp.concatenate(spread, axis=0), ALONG_J)
 
 
 def split_weights(dist, packed):
@@ -277,7 +292,8 @@
 
     def build(step, carry):
         at = pl.ds(step * group, group)
-        left[at], right[at], sums[at] = features(pts[at])
+        packs = pl.ds(step * (group // PACK), group // PACK)
+        left[packs], right[at], sums[at] = features(pts[at])
         return carry
 
     lax.fori_loop(0, blocks // group, build, 0)
@@ -308,55 +324,32 @@
         return LANES * shifted
 
     def measure(first):
-        for u in range(0, LANES, 2):
-            f, g = [], []
-            for v in (u, u + 1):
-                f.append(left[tab[1, first + v]])
-                g.append(right[tab[0, first + v]])
-            blank = jnp.zeros_like(g[0])
-            lhs = jnp.concatenate(f, axis=0)
-            rhs = jnp.concatenate(
-                [
-                    jnp.concatenate([g[0], blank], axis=1),
-                    jnp.concatenate([blank, g[1]], axis=1),
-                ],
-                axis=0,
-            )
-            dists[u // 2] = distance(lhs, rhs)
+        for u in range(LANES):
+            b = tab[1, first + u]
+            dists[u] = distance(left[lax.div(b, PACK)], right[tab[0, first + u]], lax.rem(b, PACK))
 
     def weigh(first):
         for u in range(LANES):
-            cols = slice((u % 2) * width, (u % 2 + 1) * width)
-            s_hi, l_hi, s_lo, l_lo = split_weights(dists[u // 2, :, cols], masks[first + u])
-            weights[u // 2, 0, 0:width, cols] = s_hi
-            weights[u // 2, 0, width:, cols] = l_hi
-            weights[u // 2, 1, 0:width, cols] = s_lo
-            weights[u // 2, 1, width:, cols] = l_lo
+            s_hi, l_hi, s_lo, l_lo = split_weights(dists[u], masks[first + u])
+            weights[u, 0, 0:width] = s_hi
+            weights[u, 0, width:] = l_hi
+            weights[u, 1, 0:width] = s_lo
+            weights[u, 1, width:] = l_lo
 
     def add(first):
-        for u in range(0, LANES, 2):
-            ids = [[tab[side, first + v] for v in (u, u + 1)] for side in range(2)]
-            v_a = jnp.concatenate([sums[at] for at in ids[0]], axis=0)
-            v_b = jnp.concatenate([sums[at] for at in ids[1]], axis=0)
+        for u in range(LANES):
+            a = tab[0, first + u]
+            b = tab[1, first + u]
             on_a = on_b = None
             for piece in range(2):
-                w = weights[u // 2, piece]
-                turned = jnp.concatenate(
-                    [
-                        jnp.concatenate([w[:width, :width], w[width:, :width]], axis=1),
-                        jnp.concatenate([w[:width, width:], w[width:, width:]], axis=1),
-                    ],
-                    axis=0,
-                )
-                part_a = dot(v_b, w, ALONG_J)
-                part_b = dot(v_a, turned, ALONG_I)
+                w = weights[u, piece]
+                turned = jnp.concatenate([w[:width], w[width:]], axis=1)
+                part_a = dot(sums[b], w, ALONG_J)
+                part_b = dot(sums[a], turned, ALONG_I)
                 on_a = part_a if on_a is None else on_a + part_a
                 on_b = part_b if on_b is None else on_b + part_b
-            for v in range(2):
-                rows16 = slice(16 * v, 16 * v + 16)
-                cols = slice(v * width, (v + 1) * width)
-                aterm[first + u + v] = combine(pts[ids[0][v]], on_a[rows16, cols])
-                bterm[first + u + v] = combine(pts[ids[1][v]], on_b[rows16, cols])
+            aterm[first + u] = combine(pts[a], on_a)
+            bterm[first + u] = combine(pts[b], on_b)
 
     def body(i, carry):
         @pl.when(i == begin)
@@ -368,7 +361,8 @@
                     block = got[o, step * group : (step + 1) * group]
                     to = pl.ds(blocks + o * per + step * group, group)
                     pts[to] = block
-                    left[to], _, sums[to] = features(block)
+                    packs = pl.ds((blocks + o * per + step * group) // PACK, group // PACK)
+                    left[packs], _, sums[to] = features(block)
 
         @pl.when(i == done + 2)
         def _():
@@ -518,14 +512,14 @@
                 pltpu.VMEM((3, per, 8, width), F32),
                 pltpu.VMEM((nbulk * mig, 16, width), F32),
                 pltpu.VMEM((nbulk * mig, 16, width), F32),
-                pltpu.VMEM((held, 48, width), BF16),
-                pltpu.VMEM((blocks, 48, width), BF16),
+                pltpu.VMEM((held // PACK, width, PACK * 32), BF16),
+                pltpu.VMEM((blocks, 32, width), BF16),
                 pltpu.VMEM((held, 16, 2 * width), BF16),
                 pltpu.SMEM((2, tiles), jnp.int32),
                 pltpu.VMEM((tiles, 8, width), F32),
                 pltpu.VMEM((tiles, 8, width), F32),
-                pltpu.VMEM((LANES // 2, width, 2 * width), F32),
-                pltpu.VMEM((LANES // 2, 2, 2 * width, 2 * width), BF16),
+                pltpu.VMEM((LANES, width, width), F32),
+                pltpu.VMEM((LANES, 2, 2 * width, width), BF16),
                 dma((13,)),
                 dma((3, nbulk)),
                 dma((3, nbulk)),

time: 32.2 us -> 32 us (level)
  no operation moved by 1% of the time
where the time goes in v5:
time: 32 us; the launch traced here: 31.8 us
  Pallas kernels  28.1 us (88%)
  local copies, waits for them, and re-layouts  3.01 us (9%)
  between operations  0.65 us (2%)
    pallas_call x1, Pallas kernels, per_device(): pl.pallas_call(functools.partial(kernel, nreg, nbulk), out_shape=(jax.Sha...  28.1 us
    unnamed x7, local copies, waits for them, and re-layouts  3.01 us

profile of v5, /device:TPU:0, one launch (start us, length us, event | category | flops | bytes accessed | tf_op | source)
XLA Modules:
  0.0 31.8 jit_solution(8689785216416837650)
XLA Ops:
  0.6 28.1 %shard_map.121 = (f32[64,4,128]{2,1,0:T(4,128)}, f32[3,64,128]{2,1,0:T(8,128)}, f32[11,8,128]{2,1,0:T(8,128)}) custom-call(f32[3,64,128]{2,1,0:T(8,128)} %bitcast.16, f32[64,4,128]{2,1,0:T(4,128)} %fld_hbm.1, f32[64,128]{1,0:T(8,128)} %sto_hbm.1, f32[3,64,128]{2,1,0:T(8,128)} %bitcast.17, s32[3,1,8]{2,1,0:T(1,128)} %bitcast.20, s32[2,24]{1,0:T(2,128)} %bitcast.21, ...), custom_call_target="tpu_custom_call" | custom-call | tf_op jit(solution)/shard_map/pallas_call | solution.py:486
  28.8 0.0 copy-start
  28.8 1.6 %copy.16 = f32[64,4,128]{2,1,0:T(4,128)} copy(f32[64,4,128]{2,1,0:T(4,128)} %get-tuple-element.12) | data formatting | bytes 262144
  30.4 0.0 copy-done
  30.4 0.0 copy-start.1
  30.4 0.6 %copy.17 = f32[64,3,128]{2,0,1:T(8,128)} copy(f32[64,3,128]{2,0,1:T(8,128)S(1)} %bitcast.18) | data formatting | bytes 196608
  31.0 0.1 copy-done.1
  31.2 0.6 %copy.18 = f32[8,11,128]{2,0,1:T(8,128)} copy(f32[8,11,128]{2,0,1:T(8,128)S(1)} %bitcast.19) | data formatting | bytes 90112
Async XLA Ops:
  28.8 1.6 %copy-start = (f32[3,64,128]{2,1,0:T(8,128)S(1)}, f32[3,64,128]{2,1,0:T(8,128)}, u32[]{:S(2)}) copy-start(f32[3,64,128]{2,1,0:T(8,128)} %get-tuple-element.7) | copy-start | bytes 294916
  30.4 0.8 %copy-start.1 = (f32[11,8,128]{2,1,0:T(8,128)S(1)}, f32[11,8,128]{2,1,0:T(8,128)}, u32[]{:S(2)}) copy-start(f32[11,8,128]{2,1,0:T(8,128)} %get-tuple-element.8) | copy-start | bytes 135172

commit v6 on v5

--- a/solution.py
+++ b/solution.py
@@ -150,6 +150,9 @@
     move_hbm,
     rmask_hbm,
     lmask_hbm,
+    nf_hbm,
+    nv_hbm,
+    arr_hbm,
     nf_ref,
     nv_ref,
     arr_ref,
@@ -175,12 +178,12 @@
     left,
     right,
     sums,
-    tab,
-    aterm,
+    terms,
     bterm,
     dists,
     weights,
     load_sem,
+    out_sem,
     send1,
     recv1,
     send2,
@@ -208,6 +211,10 @@
                 continue
             peers.append((o, lax.rem(me + step, nbulk)))
 
+    barrier = pltpu.get_barrier_semaphore()
+    for o, d in peers:
+        pl.semaphore_signal(barrier, inc=1, device_id=(region_at(o - 1), d), device_id_type=MESH)
+
     loads = {}
     for n, (name, src, dst) in enumerate(
         (
@@ -229,10 +236,6 @@
         loads[name] = pltpu.make_async_copy(src, dst, load_sem.at[n])
         loads[name].start()
 
-    barrier = pltpu.get_barrier_semaphore()
-    for o, d in peers:
-        pl.semaphore_signal(barrier, inc=1, device_id=(region_at(o - 1), d), device_id_type=MESH)
-
     loads["pos"].wait()
     loads["fld"].wait()
     for k in range(3):
@@ -284,10 +287,6 @@
     def arrival(ref, sem, o, b):
         pltpu.make_async_copy(span(ref, o, b), span(ref, o, b), sem.at[o, b]).wait()
 
-    pl.semaphore_wait(barrier, len(peers))
-    for o, d in peers:
-        copy1(o, d).start()
-
     group = 8
 
     def build(step, carry):
@@ -298,15 +297,12 @@
 
     lax.fori_loop(0, blocks // group, build, 0)
 
+    pl.semaphore_wait(barrier, len(peers))
+    for o, d in peers:
+        copy1(o, d).start()
+
     loads["pair_s"].wait()
     loads["touch_s"].wait()
-    for t in range(pairs):
-        tab[0, t] = pair_s[0, t]
-        tab[1, t] = pair_s[1, t]
-    for q in range(recv_count):
-        for t in range(touch):
-            tab[0, pairs + touch * q + t] = touch_s[t, q]
-            tab[1, pairs + touch * q + t] = blocks + q
     loads["lmask"].wait()
     loads["rmask"].wait()
 
@@ -323,23 +319,43 @@
         )
         return LANES * shifted
 
+    tiles = pairs + touch * recv_count
+
+    def members(first):
+        remote = first >= pairs
+        near = jnp.minimum(first, pairs - LANES)
+        far = jnp.maximum(first - pairs, 0)
+        t = far // recv_count
+        q = far % recv_count
+        found = []
+        for u in range(LANES):
+            found.append(
+                (
+                    jnp.where(remote, touch_s[t, q + u], pair_s[0, near + u]),
+                    jnp.where(remote, blocks + q + u, pair_s[1, near + u]),
+                    jnp.where(remote, pairs + touch * (q + u) + t, near + u),
+                    first + u,
+                )
+            )
+        return found
+
     def measure(first):
-        for u in range(LANES):
-            b = tab[1, first + u]
-            dists[u] = distance(left[lax.div(b, PACK)], right[tab[0, first + u]], lax.rem(b, PACK))
+        for u, (a, b, _, _) in enumerate(members(first)):
+            dists[u] = distance(left[lax.div(b, PACK)], right[a], lax.rem(b, PACK))
 
     def weigh(first):
-        for u in range(LANES):
-            s_hi, l_hi, s_lo, l_lo = split_weights(dists[u], masks[first + u])
+        for u, (_, _, m, _) in enumerate(members(first)):
+            s_hi, l_hi, s_lo, l_lo = split_weights(dists[u], masks[m])
             weights[u, 0, 0:width] = s_hi
             weights[u, 0, width:] = l_hi
             weights[u, 1, 0:width] = s_lo
             weights[u, 1, width:] = l_lo
 
+    def put(at, value):
+        terms[:, pl.ds(at, 1), :] = value[0:4].reshape(4, 1, width)
+
     def add(first):
-        for u in range(LANES):
-            a = tab[0, first + u]
-            b = tab[1, first + u]
+        for u, (a, b, _, n) in enumerate(members(first)):
             on_a = on_b = None
             for piece in range(2):
                 w = weights[u, piece]
@@ -348,8 +364,10 @@
                 part_b = dot(sums[a], turned, ALONG_I)
                 on_a = part_a if on_a is None else on_a + part_a
                 on_b = part_b if on_b is None else on_b + part_b
-            aterm[first + u] = combine(pts[a], on_a)
-            bterm[first + u] = combine(pts[b], on_b)
+            put(n, combine(pts[a], on_a))
+            term = combine(pts[b], on_b)
+            put(tiles + n, term)
+            bterm[n] = term
 
     def body(i, carry):
         @pl.when(i == begin)
@@ -368,8 +386,8 @@
         def _():
             for o in range(3):
                 for s in range(per):
-                    at = pairs + touch * (o * per + s)
-                    back[o, s] = sum(bterm[at + t] for t in range(touch))
+                    at = pairs + o * per + s
+                    back[o, s] = sum(bterm[at + t * recv_count] for t in range(touch))
             for o, d in peers:
                 copy2(o, d).start()
 
@@ -385,13 +403,18 @@
     loads["send_v"].wait()
     loads["touch_v"].wait()
     loads["pair_v"].wait()
-    used = 2 * pairs + (touch + 1) * recv_count
-    rows = -(-used // 128) * 128
+    used = 2 * tiles + recv_count
+    rows = terms.shape[1]
+
+    def none(n):
+        return jnp.full((1, n), -1, jnp.int32)
+
     index = jnp.concatenate(
-        [pair_v[0:1], pair_v[1:2]]
+        [pair_v[0:1]]
         + [touch_v[t : t + 1] for t in range(touch)]
+        + [pair_v[1:2], none(touch * recv_count)]
         + [send_v[o, s : s + 1] for o in range(3) for s in range(slots)]
-        + [jnp.full((1, rows - used), -1, jnp.int32)],
+        + [none(rows - used)],
         axis=1,
     )
     here = lax.broadcasted_iota(jnp.int32, (blocks, rows), 0)
@@ -399,20 +422,14 @@
     for o, d in peers:
         arrival(ret, recv2, o, d)
 
-    def plane(k):
-        found = [aterm[0:pairs, k, :], bterm[0:pairs, k, :]]
-        found += [aterm[pl.ds(pairs + t, recv_count, touch), k, :] for t in range(touch)]
-        if slots == 1:
-            found += [ret[o, :, k, :] for o in range(3)]
-        else:
-            found += [
-                ret[o, pl.ds(s, nbulk, slots), k, :] for o in range(3) for s in range(slots)
-            ]
-        return jnp.concatenate(found + [jnp.zeros((rows - used, width), F32)], axis=0)
-
+    for o in range(3):
+        for s in range(slots):
+            for d in range(nbulk):
+                put(2 * tiles + (o * slots + s) * nbulk + d, ret[o, d * slots + s])
+    terms[:, used:, :] = jnp.zeros((4, rows - used, width), F32)
     totals = []
     for k in range(4):
-        parts = split3(plane(k))
+        parts = split3(terms[k])
         totals.append(
             sum(jnp.dot(pick, part.astype(BF16), preferred_element_type=F32) for part in parts)
         )
@@ -424,6 +441,14 @@
         nf_ref[:, k, :] = fld_ref[:, k, :] + time_step * speed
     nf_ref[:, 3, :] = fld_ref[:, 3, :] + time_step * totals[3] / sto_ref[...]
 
+    outs = [
+        pltpu.make_async_copy(src, dst, out_sem.at[n])
+        for n, (src, dst) in enumerate(
+            ((nf_ref, nf_hbm), (nv_ref, nv_hbm), (arr_ref, arr_hbm))
+        )
+    ]
+    outs[0].start()
+    outs[1].start()
     loads["move_s"].wait()
     for d in range(nbulk):
         for m in range(mig):
@@ -450,8 +475,20 @@
         pltpu.make_async_copy(landed, landed, recv3.at[d]).wait()
     for k in range(11):
         arr_ref[k] = mgot[:, k, :]
+    outs[2].start()
     for d in others:
         copy3(d).wait_send()
+    for out in outs:
+        out.wait()
+
+
+def hand_out(*refs):
+    sems = refs[6]
+    copies = [pltpu.make_async_copy(refs[n], refs[3 + n], sems.at[n]) for n in range(3)]
+    for copy in copies:
+        copy.start()
+    for copy in copies:
+        copy.wait()
 
 
 def solution(mesh):
@@ -477,22 +514,27 @@
         per = nbulk * slots
         tiles = pairs + touch * recv_count
         held = blocks + recv_count
+        rows = -(-(2 * tiles + recv_count) // 128) * 128
         sends = send_list[0].transpose(0, 2, 1)
         touches = remote_local[0].T
         pair_rows = local_pairs[0].T
         moves = migrate_list[0].T[:, None, :]
-        vmem = pl.BlockSpec(memory_space=pltpu.VMEM)
+        hbm = pl.BlockSpec(memory_space=pltpu.HBM)
+        out_shape = (
+            jax.ShapeDtypeStruct((blocks, 4, width), F32),
+            jax.ShapeDtypeStruct((3, blocks, width), F32),
+            jax.ShapeDtypeStruct((11, nbulk * mig, width), F32),
+        )
         dma = pltpu.SemaphoreType.DMA
-        new_fields, speed, arrived = pl.pallas_call(
+        results = pl.pallas_call(
             functools.partial(kernel, nreg, nbulk),
-            out_shape=(
-                jax.ShapeDtypeStruct((blocks, 4, width), F32),
-                jax.ShapeDtypeStruct((3, blocks, width), F32),
-                jax.ShapeDtypeStruct((11, nbulk * mig, width), F32),
-            ),
-            in_specs=[pl.BlockSpec(memory_space=pltpu.HBM)] * 10,
-            out_specs=(vmem, vmem, vmem),
+            out_shape=out_shape,
+            in_specs=[hbm] * 10,
+            out_specs=(hbm, hbm, hbm),
             scratch_shapes=[
+                pltpu.VMEM((blocks, 4, width), F32),
+                pltpu.VMEM((3, blocks, width), F32),
+                pltpu.VMEM((11, nbulk * mig, width), F32),
                 pltpu.VMEM((3, blocks, width), F32),
                 pltpu.VMEM((blocks, 4, width), F32),
                 pltpu.VMEM((blocks, width), F32),
@@ -515,12 +557,12 @@
                 pltpu.VMEM((held // PACK, width, PACK * 32), BF16),
                 pltpu.VMEM((blocks, 32, width), BF16),
                 pltpu.VMEM((held, 16, 2 * width), BF16),
-                pltpu.SMEM((2, tiles), jnp.int32),
-                pltpu.VMEM((tiles, 8, width), F32),
+                pltpu.VMEM((4, rows, width), F32),
                 pltpu.VMEM((tiles, 8, width), F32),
                 pltpu.VMEM((LANES, width, width), F32),
                 pltpu.VMEM((LANES, 2, 2 * width, width), BF16),
                 dma((13,)),
+                dma((3,)),
                 dma((3, nbulk)),
                 dma((3, nbulk)),
                 dma((3, nbulk)),
@@ -543,6 +585,14 @@
             remote_mask[0].reshape((touch * recv_count,) + remote_mask.shape[3:]),
             local_mask[0],
         )
+        new_fields, speed, arrived = pl.pallas_call(
+            hand_out,
+            out_shape=out_shape,
+            in_specs=[hbm] * 3,
+            out_specs=(hbm, hbm, hbm),
+            scratch_shapes=[dma((3,))],
+            compiler_params=pltpu.CompilerParams(vmem_limit_bytes=64 << 20),
+        )(*results)
         return new_fields, speed.transpose(1, 0, 2), arrived.transpose(1, 0, 2)
 
     both = ("region", "bulk")

time: 32 us -> 38.2 us (1.19)
  Pallas kernels: 28.1 us -> 37.4 us
  local copies, waits for them, and re-layouts: 3.01 us -> 0 us
    pallas_call x1 -> x2, Pallas kernels: 28.1 us -> 37.4 us  [the longest x1 27.9 us: per_device(): pl.pallas_call(functools.partial(kernel, nreg, nbulk), out_shape=out_shap...]
    unnamed x7 -> x0, local copies, waits for them, and re-layouts: 3.01 us -> none
where the time goes in v6:
time: 38.2 us; the launch traced here: 38 us
  Pallas kernels  37.4 us (98%)
  between operations  0.64 us (2%)
    pallas_call x1, Pallas kernels, per_device(): pl.pallas_call(functools.partial(kernel, nreg, nbulk), out_shape=out_shap...  27.9 us
    pallas_call x1, Pallas kernels, per_device(): pl.pallas_call(hand_out, out_shape=out_shape, in_specs=[hbm] * 3, out_spe...  9.44 us

profile of v6, /device:TPU:0, one launch (start us, length us, event | category | flops | bytes accessed | tf_op | source)
XLA Modules:
  0.0 38.0 jit_solution(11203725483176195536)
XLA Ops:
  0.6 27.9 %shard_map.121 = (f32[64,4,128]{2,1,0:T(4,128)}, f32[3,64,128]{2,1,0:T(8,128)}, f32[11,8,128]{2,1,0:T(8,128)}) custom-call(f32[3,64,128]{2,1,0:T(8,128)} %bitcast.16, f32[64,4,128]{2,1,0:T(4,128)} %fld_hbm.1, f32[64,128]{1,0:T(8,128)} %sto_hbm.1, f32[3,64,128]{2,1,0:T(8,128)} %bitcast.17, s32[3,1,8]{2,1,0:T(1,128)} %bitcast.18, s32[2,24]{1,0:T(2,128)} %bitcast.19, ...), custom_call_target="tpu_custom_call" | custom-call | tf_op jit(solution)/shard_map/pallas_call | solution.py:529
  28.6 9.4 %shard_map.122 = (f32[64,4,128]{2,1,0:T(4,128)}, f32[3,64,128]{2,1,0:T(8,128)}, f32[11,8,128]{2,1,0:T(8,128)}) custom-call(f32[64,4,128]{2,1,0:T(4,128)} %get-tuple-element.9.refs_0_, f32[3,64,128]{2,1,0:T(8,128)} %get-tuple-element.10.refs_1_, f32[11,8,128]{2,1,0:T(8,128)} %get-tuple-element.11.refs_2_), custom_call_target="tpu_custom_call" | custom-call | tf_op jit(solution)/shard_map/pallas_call | solution.py:588

commit v7 on v6

--- a/solution.py
+++ b/solution.py
@@ -12,7 +12,7 @@
 leak_gain = 0.5
 time_step = 0.5
 half_press = 0.025
-LANES = 8
+LANES = 4
 PACK = 4
 F32 = jnp.float32
 BF16 = jnp.bfloat16
@@ -58,7 +58,8 @@
         blank,
     ]
     flat = jnp.concatenate(b_rows, axis=-2).reshape(-1, PACK * 32, block.shape[-1])
-    left = jnp.stack([flat[n].T for n in range(flat.shape[0])]).astype(BF16)
+    turned = [flat[n].T.astype(BF16) for n in range(flat.shape[0])]
+    left = jnp.stack([t[:, 32 * m : 32 * m + 32] for t in turned for m in range(PACK)])
     right = jnp.concatenate(a_rows, axis=-2).astype(BF16)
     press = block[..., 6:7, :]
     moved = roll(block, -3)
@@ -116,9 +117,8 @@
 dot = functools.partial(lax.dot_general, preferred_element_type=F32)
 
 
-def distance(left_b, right_a, part):
-    spread = [jnp.where(part == k, right_a, jnp.zeros_like(right_a)) for k in range(PACK)]
-    return dot(left_b, jnp.concatenate(spread, axis=0), ALONG_J)
+def distance(left_b, right_a):
+    return dot(left_b, right_a, ALONG_J)
 
 
 def split_weights(dist, packed):
@@ -247,19 +247,19 @@
     for o in range(3):
         for s in range(slots):
             for d in range(nbulk):
-                stage[o, d * slots + s] = pts[send_s[o, s, d]]
+                stage[o * per + d * slots + s] = pts[send_s[o, s, d]]
     for s in range(slots):
-        got[1, me * slots + s] = stage[1, me * slots + s]
+        got[per + me * slots + s] = stage[per + me * slots + s]
 
     def span(ref, o, d):
-        return ref.at[o, pl.ds(d * slots, slots)]
+        return ref.at[pl.ds(o * per + d * slots, slots)]
 
     def copy1(o, d):
         return pltpu.make_async_remote_copy(
             src_ref=span(stage, o, d),
             dst_ref=span(got, o, me),
-            send_sem=send1.at[o, d],
-            recv_sem=recv1.at[o, me],
+            send_sem=send1,
+            recv_sem=recv1,
             device_id=(region_at(o - 1), d),
             device_id_type=MESH,
         )
@@ -268,8 +268,8 @@
         return pltpu.make_async_remote_copy(
             src_ref=span(back, o, b),
             dst_ref=span(ret, o, me),
-            send_sem=send2.at[o, b],
-            recv_sem=recv2.at[o, me],
+            send_sem=send2,
+            recv_sem=recv2,
             device_id=(region_at(1 - o), b),
             device_id_type=MESH,
         )
@@ -278,21 +278,21 @@
         return pltpu.make_async_remote_copy(
             src_ref=mstage.at[pl.ds(d * mig, mig)],
             dst_ref=mgot.at[pl.ds(me * mig, mig)],
-            send_sem=send3.at[d],
-            recv_sem=recv3.at[me],
+            send_sem=send3,
+            recv_sem=recv3,
             device_id=(r, d),
             device_id_type=MESH,
         )
 
-    def arrival(ref, sem, o, b):
-        pltpu.make_async_copy(span(ref, o, b), span(ref, o, b), sem.at[o, b]).wait()
+    def await_all(ref, count, sem):
+        whole = ref.at[pl.ds(0, count)]
+        pltpu.make_async_copy(whole, whole, sem).wait()
 
     group = 8
 
     def build(step, carry):
         at = pl.ds(step * group, group)
-        packs = pl.ds(step * (group // PACK), group // PACK)
-        left[packs], right[at], sums[at] = features(pts[at])
+        left[at], right[at], sums[at] = features(pts[at])
         return carry
 
     lax.fori_loop(0, blocks // group, build, 0)
@@ -341,7 +341,7 @@
 
     def measure(first):
         for u, (a, b, _, _) in enumerate(members(first)):
-            dists[u] = distance(left[lax.div(b, PACK)], right[a], lax.rem(b, PACK))
+            dists[u] = distance(left[b], right[a])
 
     def weigh(first):
         for u, (_, _, m, _) in enumerate(members(first)):
@@ -372,22 +372,19 @@
     def body(i, carry):
         @pl.when(i == begin)
         def _():
-            for o, d in peers:
-                arrival(got, recv1, o, d)
-            for o in range(3):
-                for step in range(per // group):
-                    block = got[o, step * group : (step + 1) * group]
-                    to = pl.ds(blocks + o * per + step * group, group)
-                    pts[to] = block
-                    packs = pl.ds((blocks + o * per + step * group) // PACK, group // PACK)
-                    left[packs], _, sums[to] = features(block)
+            await_all(got, len(peers) * slots, recv1)
+            for step in range(recv_count // group):
+                block = got[step * group : (step + 1) * group]
+                to = pl.ds(blocks + step * group, group)
+                pts[to] = block
+                left[to], _, sums[to] = features(block)
 
         @pl.when(i == done + 2)
         def _():
             for o in range(3):
                 for s in range(per):
                     at = pairs + o * per + s
-                    back[o, s] = sum(bterm[at + t * recv_count] for t in range(touch))
+                    back[o * per + s] = sum(bterm[at + t * recv_count] for t in range(touch))
             for o, d in peers:
                 copy2(o, d).start()
 
@@ -398,7 +395,7 @@
 
     lax.fori_loop(0, count + 2, body, 0)
     for s in range(slots):
-        ret[1, me * slots + s] = back[1, me * slots + s]
+        ret[per + me * slots + s] = back[per + me * slots + s]
 
     loads["send_v"].wait()
     loads["touch_v"].wait()
@@ -419,13 +416,12 @@
     )
     here = lax.broadcasted_iota(jnp.int32, (blocks, rows), 0)
     pick = jnp.where(here == index, 1.0, 0.0).astype(BF16)
-    for o, d in peers:
-        arrival(ret, recv2, o, d)
+    await_all(ret, len(peers) * slots, recv2)
 
     for o in range(3):
         for s in range(slots):
             for d in range(nbulk):
-                put(2 * tiles + (o * slots + s) * nbulk + d, ret[o, d * slots + s])
+                put(2 * tiles + (o * slots + s) * nbulk + d, ret[o * per + d * slots + s])
     terms[:, used:, :] = jnp.zeros((4, rows - used, width), F32)
     totals = []
     for k in range(4):
@@ -467,27 +463,27 @@
         copy3(d).start()
     for m in range(mig):
         mgot[me * mig + m] = mstage[me * mig + m]
-    for o, d in peers:
-        copy1(o, d).wait_send()
-        copy2(o, d).wait_send()
-    for d in others:
-        landed = mgot.at[pl.ds(d * mig, mig)]
-        pltpu.make_async_copy(landed, landed, recv3.at[d]).wait()
+    await_all(stage, len(peers) * slots, send1)
+    await_all(back, len(peers) * slots, send2)
+    await_all(mgot, len(others) * mig, recv3)
     for k in range(11):
         arr_ref[k] = mgot[:, k, :]
     outs[2].start()
-    for d in others:
-        copy3(d).wait_send()
+    await_all(mstage, len(others) * mig, send3)
     for out in outs:
         out.wait()
 
 
 def hand_out(*refs):
-    sems = refs[6]
-    copies = [pltpu.make_async_copy(refs[n], refs[3 + n], sems.at[n]) for n in range(3)]
-    for copy in copies:
+    sems = refs[9]
+    into = [pltpu.make_async_copy(refs[n], refs[6 + n], sems.at[n]) for n in range(3)]
+    out = [pltpu.make_async_copy(refs[6 + n], refs[3 + n], sems.at[3 + n]) for n in range(3)]
+    for copy in into:
         copy.start()
-    for copy in copies:
+    for n in range(3):
+        into[n].wait()
+        out[n].start()
+    for copy in out:
         copy.wait()
 
 
@@ -548,13 +544,13 @@
                 pltpu.VMEM(pair_rows.shape, jnp.int32),
                 pltpu.VMEM((tiles,) + local_mask.shape[2:], jnp.int32),
                 pltpu.VMEM((held, 8, width), F32),
-                pltpu.VMEM((3, per, 8, width), F32),
-                pltpu.VMEM((3, per, 8, width), F32),
-                pltpu.VMEM((3, per, 8, width), F32),
-                pltpu.VMEM((3, per, 8, width), F32),
+                pltpu.VMEM((recv_count, 8, width), F32),
+                pltpu.VMEM((recv_count, 8, width), F32),
+                pltpu.VMEM((recv_count, 8, width), F32),
+                pltpu.VMEM((recv_count, 8, width), F32),
                 pltpu.VMEM((nbulk * mig, 16, width), F32),
                 pltpu.VMEM((nbulk * mig, 16, width), F32),
-                pltpu.VMEM((held // PACK, width, PACK * 32), BF16),
+                pltpu.VMEM((held, width, 32), BF16),
                 pltpu.VMEM((blocks, 32, width), BF16),
                 pltpu.VMEM((held, 16, 2 * width), BF16),
                 pltpu.VMEM((4, rows, width), F32),
@@ -563,12 +559,12 @@
                 pltpu.VMEM((LANES, 2, 2 * width, width), BF16),
                 dma((13,)),
                 dma((3,)),
-                dma((3, nbulk)),
-                dma((3, nbulk)),
-                dma((3, nbulk)),
-                dma((3, nbulk)),
-                dma((nbulk,)),
-                dma((nbulk,)),
+                dma,
+                dma,
+                dma,
+                dma,
+                dma,
+                dma,
             ],
             compiler_params=pltpu.CompilerParams(
                 collective_id=0, has_side_effects=True, vmem_limit_bytes=64 << 20
@@ -590,7 +586,7 @@
             out_shape=out_shape,
             in_specs=[hbm] * 3,
             out_specs=(hbm, hbm, hbm),
-            scratch_shapes=[dma((3,))],
+            scratch_shapes=[pltpu.VMEM(o.shape, F32) for o in out_shape] + [dma((6,))],
             compiler_params=pltpu.CompilerParams(vmem_limit_bytes=64 << 20),
         )(*results)
         return new_fields, speed.transpose(1, 0, 2), arrived.transpose(1, 0, 2)

time: 38.2 us -> 29.5 us (0.77)
  Pallas kernels: 37.4 us -> 28.7 us
    pallas_call x1, Pallas kernels: 9.44 us -> 1.66 us  [per_device(): pl.pallas_call(hand_out, out_shape=out_shape, in_specs=[hbm] * 3, out_spe...]
    pallas_call x1, Pallas kernels: 27.9 us -> 27 us  [per_device(): pl.pallas_call(functools.partial(kernel, nreg, nbulk), out_shape=out_shap...]
where the time goes in v7:
time: 29.5 us; the launch traced here: 29.3 us
  Pallas kernels  28.7 us (97%)
  between operations  0.64 us (2%)
    pallas_call x1, Pallas kernels, per_device(): pl.pallas_call(functools.partial(kernel, nreg, nbulk), out_shape=out_shap...  27 us
    pallas_call x1, Pallas kernels, per_device(): pl.pallas_call(hand_out, out_shape=out_shape, in_specs=[hbm] * 3, out_spe...  1.66 us

profile of v7, /device:TPU:0, one launch (start us, length us, event | category | flops | bytes accessed | tf_op | source)
XLA Modules:
  0.0 29.3 jit_solution(16772480886744334414)
XLA Ops:
  0.6 27.0 %shard_map.121 = (f32[64,4,128]{2,1,0:T(4,128)}, f32[3,64,128]{2,1,0:T(8,128)}, f32[11,8,128]{2,1,0:T(8,128)}) custom-call(f32[3,64,128]{2,1,0:T(8,128)} %bitcast.16, f32[64,4,128]{2,1,0:T(4,128)} %fld_hbm.1, f32[64,128]{1,0:T(8,128)} %sto_hbm.1, f32[3,64,128]{2,1,0:T(8,128)} %bitcast.17, s32[3,1,8]{2,1,0:T(1,128)} %bitcast.18, s32[2,24]{1,0:T(2,128)} %bitcast.19, ...), custom_call_target="tpu_custom_call" | custom-call | tf_op jit(solution)/shard_map/pallas_call | solution.py:525
  27.6 1.7 %shard_map.122 = (f32[64,4,128]{2,1,0:T(4,128)}, f32[3,64,128]{2,1,0:T(8,128)}, f32[11,8,128]{2,1,0:T(8,128)}) custom-call(f32[64,4,128]{2,1,0:T(4,128)} %get-tuple-element.9.refs_0_, f32[3,64,128]{2,1,0:T(8,128)} %get-tuple-element.10.refs_1_, f32[11,8,128]{2,1,0:T(8,128)} %get-tuple-element.11.refs_2_), custom_call_target="tpu_custom_call" | custom-call | tf_op jit(solution)/shard_map/pallas_call | solution.py:584

commit v8 on v7

--- a/solution.py
+++ b/solution.py
@@ -205,7 +205,7 @@
         return lax.rem(r + by + nreg, nreg)
 
     peers = []
-    for o in (0, 2, 1):
+    for o in range(3):
         for step in range(nbulk):
             if o == 1 and step == 0:
                 continue
@@ -259,15 +259,18 @@
             src_ref=span(stage, o, d),
             dst_ref=span(got, o, me),
             send_sem=send1,
-            recv_sem=recv1,
+            recv_sem=recv1.at[o],
             device_id=(region_at(o - 1), d),
             device_id_type=MESH,
         )
 
-    def copy2(o, b):
+    def copy2(q):
+        o = q // per
+        b = q % per // slots
+        s = q % slots
         return pltpu.make_async_remote_copy(
-            src_ref=span(back, o, b),
-            dst_ref=span(ret, o, me),
+            src_ref=back.at[pl.ds(q, 1)],
+            dst_ref=ret.at[pl.ds(o * per + me * slots + s, 1)],
             send_sem=send2,
             recv_sem=recv2,
             device_id=(region_at(1 - o), b),
@@ -288,6 +291,10 @@
         whole = ref.at[pl.ds(0, count)]
         pltpu.make_async_copy(whole, whole, sem).wait()
 
+    pl.semaphore_wait(barrier, len(peers))
+    for o, d in peers:
+        copy1(o, d).start()
+
     group = 8
 
     def build(step, carry):
@@ -296,10 +303,6 @@
         return carry
 
     lax.fori_loop(0, blocks // group, build, 0)
-
-    pl.semaphore_wait(barrier, len(peers))
-    for o, d in peers:
-        copy1(o, d).start()
 
     loads["pair_s"].wait()
     loads["touch_s"].wait()
@@ -370,23 +373,29 @@
             bterm[n] = term
 
     def body(i, carry):
-        @pl.when(i == begin)
+        for o in range(3):
+
+            @pl.when(i == begin + o * (per // LANES))
+            def _():
+                count = sum(slots for peer in peers if peer[0] == o)
+                await_all(got, count, recv1.at[o])
+                for step in range(o * per // group, (o + 1) * per // group):
+                    block = got[step * group : (step + 1) * group]
+                    to = pl.ds(blocks + step * group, group)
+                    pts[to] = block
+                    left[to], _, sums[to] = features(block)
+
+        last = i - 3 - (done - recv_count // LANES)
+
+        @pl.when((last >= 0) & (last < recv_count // LANES))
         def _():
-            await_all(got, len(peers) * slots, recv1)
-            for step in range(recv_count // group):
-                block = got[step * group : (step + 1) * group]
-                to = pl.ds(blocks + step * group, group)
-                pts[to] = block
-                left[to], _, sums[to] = features(block)
-
-        @pl.when(i == done + 2)
-        def _():
-            for o in range(3):
-                for s in range(per):
-                    at = pairs + o * per + s
-                    back[o * per + s] = sum(bterm[at + t * recv_count] for t in range(touch))
-            for o, d in peers:
-                copy2(o, d).start()
+            for u in range(LANES):
+                q = jnp.clip(last, 0, recv_count // LANES - 1) * LANES + u
+                back[q] = sum(bterm[pairs + q + t * recv_count] for t in range(touch))
+
+                @pl.when((q // per != 1) | (q % per // slots != me))
+                def _():
+                    copy2(q).start()
 
         add(first_tile(jnp.maximum(i - 2, 0)))
         weigh(first_tile(jnp.clip(i - 1, 0, count - 1)))
@@ -560,7 +569,7 @@
                 dma((13,)),
                 dma((3,)),
                 dma,
-                dma,
+                dma((3,)),
                 dma,
                 dma,
                 dma,

time: 29.5 us -> 30.3 us (1.027)
  Pallas kernels: 28.7 us -> 29.5 us
    pallas_call x1, Pallas kernels: 27 us -> 27.8 us  [per_device(): pl.pallas_call(functools.partial(kernel, nreg, nbulk), out_shape=out_shap...]
where the time goes in v8:
time: 30.3 us; the launch traced here: 30.1 us
  Pallas kernels  29.5 us (97%)
  between operations  0.64 us (2%)
    pallas_call x1, Pallas kernels, per_device(): pl.pallas_call(functools.partial(kernel, nreg, nbulk), out_shape=out_shap...  27.8 us
    pallas_call x1, Pallas kernels, per_device(): pl.pallas_call(hand_out, out_shape=out_shape, in_specs=[hbm] * 3, out_spe...  1.66 us

profile of v8, /device:TPU:0, one launch (start us, length us, event | category | flops | bytes accessed | tf_op | source)
XLA Modules:
  0.0 30.1 jit_solution(18285863218829488799)
XLA Ops:
  0.6 27.8 %shard_map.121 = (f32[64,4,128]{2,1,0:T(4,128)}, f32[3,64,128]{2,1,0:T(8,128)}, f32[11,8,128]{2,1,0:T(8,128)}) custom-call(f32[3,64,128]{2,1,0:T(8,128)} %bitcast.16, f32[64,4,128]{2,1,0:T(4,128)} %fld_hbm.1, f32[64,128]{1,0:T(8,128)} %sto_hbm.1, f32[3,64,128]{2,1,0:T(8,128)} %bitcast.17, s32[3,1,8]{2,1,0:T(1,128)} %bitcast.18, s32[2,24]{1,0:T(2,128)} %bitcast.19, ...), custom_call_target="tpu_custom_call" | custom-call | tf_op jit(solution)/shard_map/pallas_call | solution.py:534
  28.5 1.7 %shard_map.122 = (f32[64,4,128]{2,1,0:T(4,128)}, f32[3,64,128]{2,1,0:T(8,128)}, f32[11,8,128]{2,1,0:T(8,128)}) custom-call(f32[64,4,128]{2,1,0:T(4,128)} %get-tuple-element.9.refs_0_, f32[3,64,128]{2,1,0:T(8,128)} %get-tuple-element.10.refs_1_, f32[11,8,128]{2,1,0:T(8,128)} %get-tuple-element.11.refs_2_), custom_call_target="tpu_custom_call" | custom-call | tf_op jit(solution)/shard_map/pallas_call | solution.py:593

commit v9 on v7

--- a/solution.py
+++ b/solution.py
@@ -12,7 +12,7 @@
 leak_gain = 0.5
 time_step = 0.5
 half_press = 0.025
-LANES = 4
+LANES = 8
 PACK = 4
 F32 = jnp.float32
 BF16 = jnp.bfloat16
@@ -288,6 +288,10 @@
         whole = ref.at[pl.ds(0, count)]
         pltpu.make_async_copy(whole, whole, sem).wait()
 
+    pl.semaphore_wait(barrier, len(peers))
+    for o, d in peers:
+        copy1(o, d).start()
+
     group = 8
 
     def build(step, carry):
@@ -296,10 +300,6 @@
         return carry
 
     lax.fori_loop(0, blocks // group, build, 0)
-
-    pl.semaphore_wait(barrier, len(peers))
-    for o, d in peers:
-        copy1(o, d).start()
 
     loads["pair_s"].wait()
     loads["touch_s"].wait()

time: 29.5 us -> 29.7 us (level)
  no operation moved by 1% of the time
where the time goes in v9:
time: 29.7 us; the launch traced here: 29.5 us
  Pallas kernels  28.9 us (97%)
  between operations  0.64 us (2%)
    pallas_call x1, Pallas kernels, per_device(): pl.pallas_call(functools.partial(kernel, nreg, nbulk), out_shape=out_shap...  27.2 us
    pallas_call x1, Pallas kernels, per_device(): pl.pallas_call(hand_out, out_shape=out_shape, in_specs=[hbm] * 3, out_spe...  1.66 us

profile of v9, /device:TPU:0, one launch (start us, length us, event | category | flops | bytes accessed | tf_op | source)
XLA Modules:
  0.0 29.5 jit_solution(8552831834185938935)
XLA Ops:
  0.6 27.2 %shard_map.121 = (f32[64,4,128]{2,1,0:T(4,128)}, f32[3,64,128]{2,1,0:T(8,128)}, f32[11,8,128]{2,1,0:T(8,128)}) custom-call(f32[3,64,128]{2,1,0:T(8,128)} %bitcast.16, f32[64,4,128]{2,1,0:T(4,128)} %fld_hbm.1, f32[64,128]{1,0:T(8,128)} %sto_hbm.1, f32[3,64,128]{2,1,0:T(8,128)} %bitcast.17, s32[3,1,8]{2,1,0:T(1,128)} %bitcast.18, s32[2,24]{1,0:T(2,128)} %bitcast.19, ...), custom_call_target="tpu_custom_call" | custom-call | tf_op jit(solution)/shard_map/pallas_call | solution.py:525
  27.8 1.7 %shard_map.122 = (f32[64,4,128]{2,1,0:T(4,128)}, f32[3,64,128]{2,1,0:T(8,128)}, f32[11,8,128]{2,1,0:T(8,128)}) custom-call(f32[64,4,128]{2,1,0:T(4,128)} %get-tuple-element.9.refs_0_, f32[3,64,128]{2,1,0:T(8,128)} %get-tuple-element.10.refs_1_, f32[11,8,128]{2,1,0:T(8,128)} %get-tuple-element.11.refs_2_), custom_call_target="tpu_custom_call" | custom-call | tf_op jit(solution)/shard_map/pallas_call | solution.py:584
